TPU v7x, 512 devices: a whole 4x8x8 slice. The times are simulated.
512 devices in a mesh: inp: 2 (over core), chan: 8 (over y), tgrp: 32 (over z, x).
Axes of the slice: x: 4, y: 8, z: 8, core: 2. Of those that a mesh axis runs over, the one named last changes fastest.
Arguments:
- voltages: bfloat16 [2048, 524288], P(('inp', 'chan'), 'tgrp'), may hold values from -6 to 6
- input_flags: int32 [2048, 1024], P(('inp', 'chan')), may hold values 0 or 1
- channel_to_slot: int32 [1024], replicated, may hold values from -1 to 31, as said below
Outputs:
- visibility: float32 [32, 64, 2, 32, 1088], P('chan', ('inp', 'tgrp'))
Inputs may be any that keep to these rules, and one draw needn't show every extreme that they name: `channel_to_slot`: no slot is named by two channels. Frequency owner o holds the slots o * 4 to (o + 1) * 4 - 1 and receives between 1 and 4 channels, which fill its lowest slots; the last owner always receives 4 channels. Channels named -1 are not correlated.
All inputs are finite; a program needn't handle non-finite values. No bound on the sum of `input_flags` on one device may be relied on, other than what follows from the above.
Results may differ from a plain program's by a relative error of at most 0.0058.
Values may be sent and summed in bfloat16 or wider, within the bound.
No kernel may reach another device: no remote copies, remote signals or barrier semaphores. Data moves between devices by JAX's collectives and lax.ppermute only.
A program may use at most 64 MiB of HBM per device.

v0:
```python
import math

import jax
import jax.numpy as jnp
from jax import lax
from jax.sharding import PartitionSpec as P

FRAME_SAMPLES = 2048
NCHAN = 1024
TAPS = 4
OWNER_SLOTS = 4


def passed_along(value, axis, steps):
    count = lax.axis_size(axis)
    initial, last = (max(0, -steps), min(count, count - steps))
    return lax.ppermute(value, axis, [(source, source + steps) for source in range(initial, last)])


def window_table():
    sample = jnp.arange(TAPS * FRAME_SAMPLES, dtype=jnp.float32)
    middle = (sample + 0.5 - 0.5 * TAPS * FRAME_SAMPLES) / FRAME_SAMPLES
    hanning = 0.5 - 0.5 * jnp.cos(2.0 * math.pi * (sample + 0.5) / (TAPS * FRAME_SAMPLES))
    return (jnp.sinc(middle) * hanning).reshape(TAPS, FRAME_SAMPLES)


def slot_lookup_tables(channel_to_slot, slot_count):
    slot_numbers = jnp.arange(slot_count, dtype=jnp.int32)
    chan_ids = jnp.arange(NCHAN, dtype=jnp.int32)
    labelled_items = channel_to_slot[:, None] == slot_numbers[None, :]
    slot_channel = jnp.sum(jnp.where(labelled_items, chan_ids[:, None], 0), 0)
    slot_used = jnp.any(labelled_items, 0)
    sample = jnp.arange(FRAME_SAMPLES, dtype=jnp.int32)
    phase_angle = (slot_channel[:, None] * sample[None, :] % FRAME_SAMPLES).astype(jnp.float32) * (
        2.0 * math.pi / FRAME_SAMPLES
    )
    cosine_matrix = jnp.where(slot_used[:, None], jnp.cos(phase_angle), 0.0).astype(jnp.bfloat16)
    sine_matrix = jnp.where(slot_used[:, None], -jnp.sin(phase_angle), 0.0).astype(jnp.bfloat16)
    return (labelled_items, cosine_matrix, sine_matrix)


def filter_frames(padded, window_taps, frame_count):
    summed = window_taps[0] * padded[:, 0:frame_count, :].astype(jnp.float32)
    for offset in range(1, TAPS):
        summed = summed + window_taps[offset] * padded[:, offset : offset + frame_count, :].astype(
            jnp.float32
        )
    return summed.astype(jnp.bfloat16)


def on_device(voltages, input_flags, channel_to_slot):
    in_dev = voltages.shape[0]
    frame_count = voltages.shape[1] // FRAME_SAMPLES
    frequency_owner_list = lax.axis_size("chan")
    slot_count = frequency_owner_list * OWNER_SLOTS
    groups = lax.axis_size("tgrp")
    block_count = lax.axis_size("inp") * groups
    offsets = block_count // 2 + 2
    total_frames = frame_count * groups
    norm_scale = 1.0 / math.sqrt(total_frames)
    row_block = lax.axis_index("inp") * groups + lax.axis_index("tgrp")
    signal = voltages.reshape(in_dev, frame_count, FRAME_SAMPLES)
    history = passed_along(signal[:, frame_count - (TAPS - 1) :, :], "tgrp", 1)
    padded = jnp.concatenate([history, signal], 1)
    filtered = filter_frames(padded, window_table(), frame_count)
    labelled_items, cosine_matrix, sine_matrix = slot_lookup_tables(channel_to_slot, slot_count)
    slot_table = jnp.stack(
        [
            cosine_matrix.reshape(frequency_owner_list, OWNER_SLOTS, FRAME_SAMPLES),
            sine_matrix.reshape(frequency_owner_list, OWNER_SLOTS, FRAME_SAMPLES),
        ],
        2,
    )
    channel_spectra = jnp.einsum(
        "oqrm,ifm->oqirf", slot_table, filtered, preferred_element_type=jnp.float32
    )
    flagged_choice = jnp.dot(
        input_flags.astype(jnp.float32),
        labelled_items.astype(jnp.float32),
        precision=lax.Precision.HIGHEST,
    )
    flagged_choice = jnp.transpose(
        flagged_choice.reshape(in_dev, frequency_owner_list, OWNER_SLOTS), (1, 2, 0)
    )
    slot_placed = (channel_spectra * 0.03125 * flagged_choice[:, :, :, None, None]).astype(
        jnp.bfloat16
    )
    block_in = lax.all_to_all(slot_placed, "chan", split_axis=0, concat_axis=2, tiled=True)[0]
    item_count = block_in.shape[0]
    block_inputs = block_in.shape[1]
    row_count = block_inputs // groups
    turned = lax.all_to_all(block_in, "tgrp", split_axis=1, concat_axis=3, tiled=True)
    row_stack = turned.reshape(item_count, row_count, 2 * total_frames)
    real_part = row_stack[:, :, :total_frames]
    imag_part = row_stack[:, :, total_frames:]
    left_rows = jnp.concatenate([row_stack, jnp.concatenate([imag_part, -real_part], 2)], 1)
    product = jnp.einsum(
        "sre,sce->src",
        left_rows,
        lax.all_gather(row_stack, ("inp", "tgrp"), axis=1, tiled=True),
        preferred_element_type=jnp.float32,
    )
    first = (row_block - 1 + block_count) % block_count * row_count
    doubled = jnp.concatenate([product, product], 2)
    kept = lax.dynamic_slice_in_dim(doubled, first, offsets * row_count, 2) * norm_scale
    tiles = kept.reshape(item_count, 2, row_count, offsets * row_count)
    return tiles[:, None]


def solution(mesh):
    placed = (P(("inp", "chan"), "tgrp"), P(("inp", "chan"), None), P())
    return jax.shard_map(
        on_device,
        mesh=mesh,
        in_specs=placed,
        out_specs=P("chan", ("inp", "tgrp"), None, None, None),
        check_vma=False,
    )
```

profile of v0, /device:TPU:1, one launch (start us, length us, event | category | flops | bytes accessed | tf_op | source)
XLA Modules:
  0.0 200.1 jit_solution(7122826270688158320)
XLA Ops:
  6.5 0.0 all-gather.2.cloned.1.call-start
  6.5 0.0 copy-start.1
  6.5 2.5 %copy.95 = bf16[16,8,8,2048]{3,2,0,1:T(8,128)(2,1)S(1)} copy(bf16[16,8,8,2048]{3,2,1,0:T(8,128)(2,1)} %bitcast.50) | data formatting | bytes 8388608 | tf_op jit(solution)/shard_map/reshape | solution.py:62
  9.1 0.1 slice.45
  9.2 4.0 %collective-permute-start = (bf16[128,3,2048]{2,0,1:T(8,128)(2,1)S(1)}, bf16[128,3,2048]{2,0,1:T(8,128)(2,1)S(1)}, u32[]{:S(2)}, u32[]{:S(2)}) collective-permute-start(bf16[128,3,2048]{2,0,1:T(8,128)(2,1)S(1)} %slice.45), channel_id=1, source_target_pairs={{0,1},{1,2},{2,3},{3,4},{4,5},{5,6},{6,7},{7,8},{8,9},{9,10},{10,1... | collective-permute-start | bytes 4718600 | tf_op jit(solution)/shard_map/ppermute | solution.py:17
  13.2 0.0 copy-done.1
  13.2 0.1 select_reduce_fusion
  13.3 0.1 mul.259
  13.4 0.1 copy.70
  13.5 0.1 fusion.29
  13.6 0.1 broadcast_in_dim.43
  13.7 0.1 copy.69
  13.8 1.4 convolution_multiply_fusion
  15.3 0.2 fusion.35
  15.5 1.3 select_convert_fusion.1
  16.7 26.1 %collective-permute-done = bf16[128,3,2048]{2,0,1:T(8,128)(2,1)S(1)} collective-permute-done((bf16[128,3,2048]{2,0,1:T(8,128)(2,1)S(1)}, bf16[128,3,2048]{2,0,1:T(8,128)(2,1)S(1)}, u32[]{:S(2)}, u32[]{:S(2)}) %collective-permute-start) | collective-permute-done | bytes 1572896 | tf_op jit(solution)/shard_map/ppermute | solution.py:17
  42.8 0.1 constant_dynamic-update-slice_fusion.1
  42.9 0.0 copy-start
  43.0 2.7 %constant_dynamic-update-slice_fusion = bf16[128,11,2048]{2,0,1:T(8,128)(2,1)S(1)} fusion(bf16[128,11,2048]{2,0,1:T(8,128)(2,1)S(1)} %constant_dynamic-update-slice_fusion.1, bf16[16,8,8,2048]{3,2,1,0:T(8,128)(2,1)} %bitcast.51), kind=kLoop, calls=%fused_computation.76 | loop fusion | bytes 8388608 | tf_op jit(solution)/shard_map/concatenate | solution.py:64
  45.6 0.8 copy-done
  46.4 3.2 %fusion.11 = bf16[8,4,128,2,8]{2,0,3,1,4:T(8,128)(2,1)S(1)} fusion(bf16[128,11,2048]{2,0,1:T(8,128)(2,1)S(1)} %constant_dynamic-update-slice_fusion, f32[2048]{0:T(1024)S(1)} %get-tuple-element.8, f32[2048]{0:T(1024)S(1)} %get-tuple-element.9, f32[2048]{0:T(1024)S(1)} %get-tuple-element.10, f32[2048]{0:T(1024)S(1)} %get-tuple-element.7, ...), kind=kOutput, calls=%fused_computation.10 | convolution fusion | flops 294256640 | bytes 17219584 | tf_op jit(solution)/shard_map/oqrm,ifm->oqirf/dot_general | solution.py:74
  49.6 0.1 copy.72
  49.8 17.9 %all_to_all.30 = bf16[8,4,128,2,8]{2,3,1,4,0:T(2,128)(2,1)S(1)} all-to-all(bf16[8,4,128,2,8]{2,3,1,4,0:T(2,128)(2,1)S(1)} %copy.72), channel_id=1, replica_groups=mesh['inp'=2,'chan'=8,'tgrp'=32] {'chan'}, dimensions={0} | all-to-all | bytes 262144 | tf_op jit(solution)/shard_map/all_to_all | solution.py:88
  67.6 1.5 copy.83
  69.1 2.2 %reshape.130 = bf16[32,2,1024]{2,1,0:T(2,128)(2,1)S(1)} reshape(bf16[1024,4,2,8]{3,2,1,0:T(2,128)(2,1)S(1)} %bitcast.54) | data formatting | bytes 262144
  71.3 23.9 %all_to_all.31 = bf16[32,2,1024]{2,1,0:T(2,128)(2,1)S(1)} all-to-all(bf16[32,2,1024]{2,1,0:T(2,128)(2,1)S(1)} %reshape.130), channel_id=1, replica_groups=mesh['inp'=2,'chan'=8,'tgrp'=32] {'tgrp'}, dimensions={0} | all-to-all | bytes 262144 | tf_op jit(solution)/shard_map/all_to_all | solution.py:92
  95.2 2.4 %reshape.131 = bf16[1024,4,2,8]{3,2,1,0:T(2,128)(2,1)S(1)} reshape(bf16[32,2,1024]{2,1,0:T(2,128)(2,1)S(1)} %all_to_all.31) | data formatting | bytes 262144
  97.6 3.2 %copy.85 = bf16[4,32,32,2,8]{2,4,1,3,0:T(8,128)(2,1)S(1)} copy(bf16[4,32,32,2,8]{4,3,0,2,1:T(2,128)(2,1)S(1)} %bitcast.53) | data formatting | bytes 262144 | tf_op jit(solution)/shard_map/all_to_all | solution.py:92
  100.8 0.8 copy.79
  101.7 0.0 all-gather.2.cloned.1.call-update
  101.7 0.9 fusion.62
  102.6 82.9 %all-gather.2.cloned.1.call-done = bf16[4,2048,512]{2,1,0:T(8,128)(2,1)} async-done(((bf16[4,32,512]{2,1,0:T(8,128)(2,1)}), bf16[4,2048,512]{2,1,0:T(8,128)(2,1)}) %all-gather.2.cloned.1.call-update) | async-done | bytes 8388624 | tf_op jit(solution)/shard_map/all_gather | solution.py:100
  185.5 6.1 %fusion.20 = f32[4,64,2048]{2,1,0:T(8,128)S(1)} fusion(bf16[4,2048,512]{2,1,0:T(8,128)(2,1)} %all-gather.2.cloned.1.call-done, bf16[4,32,256]{2,1,0:T(8,128)(2,1)S(1)} %get-tuple-element.6, bf16[4,32,256]{2,1,0:T(8,128)(2,1)S(1)} %get-tuple-element.5, bf16[4,32,512]{2,1,0:T(8,128)(2,1)} %copy.79), kind=kOutput, calls=%fused_computation.22 | convolution fusion | flops 537657344 | bytes 10747904 | tf_op jit(solution)/shard_map/sre,sce->src/dot_general | solution.py:97
  191.5 1.7 fusion.4
  (2 shorter events, 0.0 us)
Async XLA Ops:
  6.5 178.9 %all-gather.2.cloned.1.call-start = ((), (), s32[]{:S(2)}) async-start(), calls=%async_computation.2 | async-start | bytes 8519680 | tf_op jit(solution)/shard_map/all_gather | solution.py:100
  6.5 6.7 %copy-start.1 = (s32[1024]{0:T(1024)S(1)}, s32[1024]{0:T(1024)}, u32[]{:S(2)}) copy-start(s32[1024]{0:T(1024)} %param.5) | copy-start | bytes 12292
  9.2 33.7 %collective-permute-start = (bf16[128,3,2048]{2,0,1:T(8,128)(2,1)S(1)}, bf16[128,3,2048]{2,0,1:T(8,128)(2,1)S(1)}, u32[]{:S(2)}, u32[]{:S(2)}) collective-permute-start(bf16[128,3,2048]{2,0,1:T(8,128)(2,1)S(1)} %slice.45), channel_id=1, source_target_pairs={{0,1},{1,2},{2,3},{3,4},{4,5},{5,6},{6,7},{7,8},{8,9},{9,10},{10,1... | collective-permute-start | bytes 4718600 | tf_op jit(solution)/shard_map/ppermute | solution.py:17
  42.9 3.5 %copy-start = (bf16[128,16384]{1,0:T(8,128)(2,1)S(1)}, bf16[128,16384]{1,0:T(8,128)(2,1)}, u32[]{:S(2)}) copy-start(bf16[128,16384]{1,0:T(8,128)(2,1)} %param.3) | copy-start | bytes 12582916
Sparse Core Ops, SparseCore 0:
  101.8 83.5 all-gather.1
where the time goes:
time: 200 us
  waiting for transfers between devices  109 us (54%)
  blocking collectives  41.7 us (21%)
  local copies, waits for them, and re-layouts  16.8 us (8%)
  between operations  13.5 us (7%)
  matrix products  10.8 us (5%)
  other arithmetic  4.27 us (2%)
  starting transfers between devices  4.05 us (2%)
    all_gather x1, waiting for transfers between devices, on_device(): lax.all_gather(row_stack, ('inp', 'tgrp'), axis=1, tiled=True)  82.9 us
    ppermute x1, waiting for transfers between devices, passed_along(): lax.ppermute(value, axis, [(source, source + steps) for source in range(i...  26.1 us
    all_to_all x1, blocking collectives, on_device(): lax.all_to_all(block_in, 'tgrp', split_axis=1, concat_axis=3, tiled=True)  23.9 us
    all_to_all x1, blocking collectives, on_device(): lax.all_to_all(slot_placed, 'chan', split_axis=0, concat_axis=2, tiled=True)  17.9 us
    dot_general x1, matrix products, on_device(): jnp.einsum('sre,sce->src', left_rows, lax.all_gather(row_stack, ('inp', '...  6.08 us
    unnamed x7, local copies, waits for them, and re-layouts  5.51 us
    ppermute x1, starting transfers between devices, passed_along(): lax.ppermute(value, axis, [(source, source + steps) for source in range(i...  4.04 us
  transfers between devices with their start and end apart: 2, of which 2 were waited for; matrix products, arithmetic and copies ran while one was open for 2% of the time, Pallas kernels for 0%

commit v1 on v0

v1 whole, which is shorter than its diff:
```python
import math

import jax
import jax.numpy as jnp
import numpy as np
from jax import lax
from jax.experimental import pallas as pl
from jax.experimental.pallas import tpu as pltpu
from jax.sharding import Mesh, PartitionSpec as P

FRAME_SAMPLES = 2048
NCHAN = 1024
TAPS = 4
SLOTS = 32
FRAMES = 8
IN_DEV = 128
LANES = 128
BLK = 32
KT = 34
ROW_TARGETS = 4
GATHER = 8
MESSAGE = 2 * FRAMES
SPECTRUM_SCALE = 2.0**-7
NT = (((1,), (1,)), ((), ()))
VMEM = pltpu.VMEM


def window_table():
    sample = np.arange(TAPS * FRAME_SAMPLES, dtype=np.float64)
    middle = (sample + 0.5 - 0.5 * TAPS * FRAME_SAMPLES) / FRAME_SAMPLES
    hanning = 0.5 - 0.5 * np.cos(2.0 * math.pi * (sample + 0.5) / (TAPS * FRAME_SAMPLES))
    return (np.sinc(middle) * hanning).reshape(TAPS, FRAME_SAMPLES).astype(np.float32)


def spectra_kernel(slots_ref, window_ref, flags_hbm, volts_hbm, spec_ref, part_ref, kept_ref, volts, table, flags, sems):
    copies = []
    for frame in range(FRAMES):
        copy = pltpu.make_async_copy(
            volts_hbm.at[:, pl.ds(frame * FRAME_SAMPLES, FRAME_SAMPLES)],
            volts.at[frame // 2, pl.ds(frame % 2 * IN_DEV, IN_DEV), :],
            sems.at[frame],
        )
        copy.start()
        copies.append(copy)
    flag_copy = pltpu.make_async_copy(flags_hbm, flags, sems.at[FRAMES])
    flag_copy.start()

    chosen = lax.broadcasted_iota(jnp.int32, (SLOTS, NCHAN), 0) == slots_ref[...]
    channel = jnp.sum(
        jnp.where(chosen, lax.broadcasted_iota(jnp.int32, (SLOTS, NCHAN), 1), 0).astype(jnp.float32), 1, keepdims=True
    ).astype(jnp.int32)
    lane = lax.broadcasted_iota(jnp.int32, (SLOTS, LANES), 1)
    turn = 2.0 * math.pi / FRAME_SAMPLES
    fine = ((channel * lane) & (FRAME_SAMPLES - 1)).astype(jnp.float32) * turn
    coarse = ((channel * (lane * LANES)) & (FRAME_SAMPLES - 1)).astype(jnp.float32) * turn
    fine_cos, fine_sin = jnp.cos(fine), jnp.sin(fine)
    coarse_cos, coarse_sin = jnp.cos(coarse), jnp.sin(coarse)
    for piece in range(FRAME_SAMPLES // LANES):
        at = pl.ds(piece * LANES, LANES)
        ccos, csin = coarse_cos[:, piece : piece + 1], coarse_sin[:, piece : piece + 1]
        cosine = (ccos * fine_cos - csin * fine_sin).astype(jnp.bfloat16).astype(jnp.float32)
        sine = (-(csin * fine_cos + ccos * fine_sin)).astype(jnp.bfloat16).astype(jnp.float32)
        for tap in range(TAPS):
            weight = window_ref[tap : tap + 1, at]
            table[pl.ds(tap * 64, 32), at] = (cosine * weight).astype(jnp.bfloat16)
            table[pl.ds(tap * 64 + 32, 32), at] = (sine * weight).astype(jnp.bfloat16)

    flag_copy.wait()
    kept_ref[...] = lax.dot_general(
        chosen.astype(jnp.float32).astype(jnp.bfloat16),
        flags[...].astype(jnp.float32).astype(jnp.bfloat16),
        NT,
        preferred_element_type=jnp.float32,
    )

    sums = {}
    for pair in range(FRAMES // 2):
        copies[2 * pair].wait()
        copies[2 * pair + 1].wait()
        terms = lax.dot_general(table[...], volts[pair], NT, preferred_element_type=jnp.float32)
        for half in range(2):
            for tap in range(TAPS):
                frame = 2 * pair + half + TAPS - 1 - tap
                term = terms[tap * 64 : tap * 64 + 64, half * IN_DEV : (half + 1) * IN_DEV]
                sums[frame] = term if frame not in sums else sums[frame] + term
        for frame in [f for f in sums if f < 2 * pair + 2]:
            done = sums.pop(frame)
            spec_ref[frame] = done[:32]
            spec_ref[FRAMES + frame] = done[32:]
    for frame, done in sums.items():
        part_ref[frame - FRAMES] = done[:32]
        part_ref[TAPS - 1 + frame - FRAMES] = done[32:]


def slotted_kernel(spec_ref, part_ref, kept_ref, out_ref, rows):
    kept = kept_ref[...]
    for frame in range(FRAMES):
        for half in range(2):
            value = spec_ref[half * FRAMES + frame]
            if frame < TAPS - 1:
                value = value + part_ref[half * (TAPS - 1) + frame]
            rows[pl.ds(half * FRAMES + frame, SLOTS, stride=MESSAGE), :] = value * kept
    out_ref[...] = rows[...].astype(jnp.bfloat16)


def product_kernel(place_ref, own_ref, other_ref, out_ref, left, prod):
    zl, x = place_ref[0], place_ref[1]
    depth = GATHER * 64
    pick = (
        lax.broadcasted_iota(jnp.int32, (BLK, LANES), 1) == lax.broadcasted_iota(jnp.int32, (BLK, LANES), 0) + BLK * x
    ).astype(jnp.float32).astype(jnp.bfloat16)
    for target in range(ROW_TARGETS):
        rows = own_ref[:, 2 * target + zl, :, :].reshape(depth, LANES)
        wide = rows.astype(jnp.float32).reshape(depth // MESSAGE, MESSAGE, LANES)
        turned = jnp.concatenate([wide[:, FRAMES:], -wide[:, :FRAMES]], 1).reshape(depth, LANES).astype(jnp.bfloat16)
        left[pl.ds(target * 64, BLK), :] = lax.dot_general(
            pick, rows, NT, preferred_element_type=jnp.float32
        ).astype(jnp.bfloat16)
        left[pl.ds(target * 64 + BLK, BLK), :] = lax.dot_general(
            pick, turned, NT, preferred_element_type=jnp.float32
        ).astype(jnp.bfloat16)
    for source, ref in enumerate((own_ref, other_ref)):
        for pair in range(4):
            right = jnp.concatenate(
                [ref[:, 2 * pair + i, :, :].reshape(depth, LANES) for i in range(2)], 1
            )
            value = jnp.dot(left[...], right, preferred_element_type=jnp.float32)
            group = source * 8 + pair * 2
            prod[:, pl.ds((group + 1) * LANES, 2 * LANES)] = value
            if group == 0:
                prod[:, pl.ds(17 * LANES, LANES)] = value[:, :LANES]
            if group == 14:
                prod[:, pl.ds(0, LANES)] = value[:, LANES:]
    first = zl + jnp.where(x == 0, 0, 1)
    shift = lax.rem(x + 3, 4) * BLK
    span = 10 * LANES
    for target in range(ROW_TARGETS):
        start = pl.multiple_of((first + 2 * target) * LANES, LANES)
        window = prod[pl.ds(target * 64, 64), pl.ds(start, span)]
        window = pltpu.roll(window, lax.rem(span - shift, span), 1)
        out_ref[target] = window[:, : KT * BLK].astype(jnp.bfloat16)


def on_device(voltages, input_flags, channel_to_slot):
    any_space = pl.BlockSpec(memory_space=pl.ANY)
    vmem = pl.BlockSpec(memory_space=VMEM)
    f32, bf16 = jnp.float32, jnp.bfloat16
    window = jnp.asarray(window_table() * np.float32(SPECTRUM_SCALE))
    spec, part, kept = pl.pallas_call(
        spectra_kernel,
        out_shape=(
            jax.ShapeDtypeStruct((MESSAGE, SLOTS, IN_DEV), f32),
            jax.ShapeDtypeStruct((2 * (TAPS - 1), SLOTS, IN_DEV), f32),
            jax.ShapeDtypeStruct((SLOTS, IN_DEV), f32),
        ),
        in_specs=[vmem, vmem, any_space, any_space],
        out_specs=(vmem, vmem, vmem),
        scratch_shapes=[
            VMEM((FRAMES // 2, 2 * IN_DEV, FRAME_SAMPLES), bf16),
            VMEM((TAPS * 64, FRAME_SAMPLES), bf16),
            VMEM((IN_DEV, NCHAN), jnp.int32),
            pltpu.SemaphoreType.DMA((FRAMES + 1,)),
        ],
        compiler_params=pltpu.CompilerParams(vmem_limit_bytes=24 * 2**20),
        name="spectra",
    )(channel_to_slot[None, :], window, input_flags, voltages)

    groups = [(i, i + 1) for i in range(31)]
    history = lax.ppermute(part, ("zh", "zl", "x"), groups)

    slotted = pl.pallas_call(
        slotted_kernel,
        out_shape=jax.ShapeDtypeStruct((SLOTS * MESSAGE, IN_DEV), bf16),
        in_specs=[vmem, vmem, vmem],
        out_specs=vmem,
        scratch_shapes=[VMEM((SLOTS * MESSAGE, IN_DEV), f32)],
        name="slotted",
    )(spec, history, kept)

    placed = lax.all_to_all(
        slotted.reshape(SLOTS, MESSAGE, IN_DEV), ("chan", "zh"), split_axis=0, concat_axis=0, tiled=True
    )
    copies = jnp.broadcast_to(placed.reshape(1, SLOTS * MESSAGE, IN_DEV), (GATHER, SLOTS * MESSAGE, IN_DEV))
    own = lax.all_to_all(copies, ("zl", "x"), split_axis=0, concat_axis=0, tiled=True)
    other = lax.ppermute(own, "inp", [(0, 1), (1, 0)])

    place = jnp.stack([lax.axis_index("zl"), lax.axis_index("x")]).astype(jnp.int32)
    blocked = (GATHER, 8, 64, LANES)
    rows = pl.pallas_call(
        product_kernel,
        out_shape=jax.ShapeDtypeStruct((ROW_TARGETS, 64, KT * BLK), bf16),
        in_specs=[pl.BlockSpec(memory_space=pltpu.SMEM), vmem, vmem],
        out_specs=vmem,
        scratch_shapes=[VMEM((256, GATHER * 64), bf16), VMEM((256, 18 * LANES), f32)],
        compiler_params=pltpu.CompilerParams(vmem_limit_bytes=24 * 2**20),
        name="products",
    )(place, own.reshape(blocked), other.reshape(blocked))

    tiles = lax.all_to_all(rows, "zh", split_axis=0, concat_axis=0, tiled=True)
    return tiles.astype(f32).reshape(ROW_TARGETS, 1, 2, BLK, KT * BLK)


def solution(mesh):
    parts = Mesh(mesh.devices.reshape(2, 8, 4, 2, 4), ("inp", "chan", "zh", "zl", "x"))
    return jax.shard_map(
        on_device,
        mesh=parts,
        in_specs=(P(("inp", "chan"), ("zh", "zl", "x")), P(("inp", "chan"), None), P()),
        out_specs=P("chan", ("inp", "zh", "zl", "x"), None, None, None),
        check_vma=False,
    )
```

time: 200 us -> 95.4 us (0.48)
  waiting for transfers between devices: 109 us -> 3.8 us
  blocking collectives: 41.7 us -> 64.4 us
  between operations: 13.5 us -> 0.06 us
  matrix products: 10.8 us -> 0 us
  local copies, waits for them, and re-layouts: 16.8 us -> 6.75 us
  Pallas kernels: 0 us -> 7.89 us
  starting transfers between devices: 4.05 us -> 10.8 us
  other arithmetic: 4.27 us -> 1.18 us
    all_gather x1 -> x0, waiting for transfers between devices: 82.9 us -> none  [on_device(): lax.all_gather(row_stack, ('inp', 'tgrp'), axis=1, tiled=True)]
    all_to_all x2 -> x3, blocking collectives: 41.7 us -> 64.4 us  [the longest x1 31 us: on_device(): lax.all_to_all(slotted.reshape(SLOTS, MESSAGE, IN_DEV), ('chan', 'zh'), s...]
    ppermute x1 -> x2, waiting for transfers between devices: 26.1 us -> 3.8 us  [the longest x1 2.18 us: on_device(): other = lax.ppermute(own, 'inp', [(0, 1), (1, 0)])]
    dot_general x3 -> x0, matrix products: 10.8 us -> none  [the longest x1 6.08 us: on_device(): jnp.einsum('sre,sce->src', left_rows, lax.all_gather(row_stack, ('inp', '...]
    pallas_call x0 -> x3, Pallas kernels: none -> 7.89 us  [the longest x1 4.11 us: on_device(): pl.pallas_call(spectra_kernel, out_shape=(jax.ShapeDtypeStruct((MESSAGE,...]
    ppermute x1 -> x2, starting transfers between devices: 4.04 us -> 10.8 us  [the longest x1 6.9 us: on_device(): other = lax.ppermute(own, 'inp', [(0, 1), (1, 0)])]
    reshape x2 -> x0, local copies, waits for them, and re-layouts: 3.35 us -> none  [the longest x1 2.51 us: on_device(): signal = voltages.reshape(in_dev, frame_count, FRAME_SAMPLES)]
    all_to_all x1 -> x0, local copies, waits for them, and re-layouts: 3.18 us -> none  [on_device(): lax.all_to_all(block_in, 'tgrp', split_axis=1, concat_axis=3, tiled=True)]
  transfers between devices with their start and end apart: 2 -> 2, of which waited for: 2 -> 2; matrix products, arithmetic and copies ran while one was open for 2% -> 0% of each run, Pallas kernels for 0% -> 0%
where the time goes in v1:
time: 95.4 us; the launch traced here: 94.9 us
  blocking collectives  64.4 us (68%)
  starting transfers between devices  10.8 us (11%)
  Pallas kernels  7.89 us (8%)
  local copies, waits for them, and re-layouts  6.75 us (7%)
  waiting for transfers between devices  3.8 us (4%)
  other arithmetic  1.18 us (1%)
    all_to_all x1, blocking collectives, on_device(): lax.all_to_all(slotted.reshape(SLOTS, MESSAGE, IN_DEV), ('chan', 'zh'), s...  31 us
    all_to_all x1, blocking collectives, on_device(): tiles = lax.all_to_all(rows, 'zh', split_axis=0, concat_axis=0, tiled=True)  19.4 us
    all_to_all x1, blocking collectives, on_device(): lax.all_to_all(copies, ('zl', 'x'), split_axis=0, concat_axis=0, tiled=True)  14 us
    ppermute x1, starting transfers between devices, on_device(): other = lax.ppermute(own, 'inp', [(0, 1), (1, 0)])  6.9 us
    unnamed x14, local copies, waits for them, and re-layouts  6.62 us
    pallas_call x1, Pallas kernels, on_device(): pl.pallas_call(spectra_kernel, out_shape=(jax.ShapeDtypeStruct((MESSAGE,...  4.11 us
    ppermute x1, starting transfers between devices, on_device(): history = lax.ppermute(part, ('zh', 'zl', 'x'), groups)  3.94 us
    ppermute x1, waiting for transfers between devices, on_device(): other = lax.ppermute(own, 'inp', [(0, 1), (1, 0)])  2.18 us
  transfers between devices with their start and end apart: 2, of which 2 were waited for; matrix products, arithmetic and copies ran while one was open for 0% of the time, Pallas kernels for 0%

profile of v1, /device:TPU:1, one launch (start us, length us, event | category | flops | bytes accessed | tf_op | source)
XLA Modules:
  0.0 94.9 jit_solution(10406071822018271643)
XLA Ops:
  0.0 0.0 copy-start
  0.0 2.2 %copy-done = bf16[128,16384]{1,0:T(8,128)(2,1)S(1)} copy-done((bf16[128,16384]{1,0:T(8,128)(2,1)S(1)}, bf16[128,16384]{1,0:T(8,128)(2,1)}, u32[]{:S(2)}) %copy-start) | copy-done | bytes 4194328
  2.2 0.0 copy-start.1
  2.2 1.0 %copy-done.1 = s32[128,1024]{1,0:T(8,128)S(1)} copy-done((s32[128,1024]{1,0:T(8,128)S(1)}, s32[128,1024]{1,0:T(8,128)}, u32[]{:S(2)}) %copy-start.1) | copy-done | bytes 524312
  3.2 0.0 copy-start.3
  3.2 0.8 copy-done.3
  4.0 0.0 copy-start.5
  4.0 0.7 copy-done.5
  4.7 4.1 %spectra.1 = (f32[16,32,128]{2,1,0:T(8,128)S(1)}, f32[6,32,128]{2,1,0:T(8,128)S(1)}, f32[32,128]{1,0:T(8,128)S(1)}) custom-call(s32[1,1024]{1,0:T(1,128)S(1)} %bitcast.14, f32[4,2048]{1,0:T(4,128)S(1)} %copy-done.3, s32[128,1024]{1,0:T(8,128)S(1)} %copy-done.1, bf16[128,16384]{1,0:T(8,128)(2,1)S(1)} %copy-done), custom_call_target="tpu_custom_call" | custom-call | tf_op jit(solution)/shard_map/spectra/pallas_call | solution.py:149
  8.8 0.0 copy-start.2
  8.8 0.7 copy-done.2
  9.5 0.0 copy-start.4
  9.5 0.6 copy-done.4
  10.1 3.9 %collective-permute-start = (f32[6,32,128]{2,1,0:T(8,128)S(1)}, f32[6,32,128]{2,1,0:T(8,128)S(1)}, u32[]{:S(2)}, u32[]{:S(2)}) collective-permute-start(f32[6,32,128]{2,1,0:T(8,128)S(1)} %get-tuple-element.9), channel_id=1, source_target_pairs={{0,1},{1,2},{2,3},{3,4},{4,5},{5,6},{6,7},{7,8},{8,9},{9,10},{10,1... | collective-permute-start | bytes 294920 | tf_op jit(solution)/shard_map/ppermute | solution.py:169
  14.0 1.6 %collective-permute-done.part_ref = f32[6,32,128]{2,1,0:T(8,128)S(1)} collective-permute-done((f32[6,32,128]{2,1,0:T(8,128)S(1)}, f32[6,32,128]{2,1,0:T(8,128)S(1)}, u32[]{:S(2)}, u32[]{:S(2)}) %collective-permute-start) | collective-permute-done | bytes 98336 | tf_op jit(solution)/shard_map/ppermute | solution.py:169
  15.7 0.0 copy-start.6
  15.7 0.6 copy-done.6
  16.3 1.8 %slotted.1 = bf16[512,128]{1,0:T(8,128)(2,1)} custom-call(f32[16,32,128]{2,1,0:T(8,128)} %copy-done.2, f32[6,32,128]{2,1,0:T(8,128)} %copy-done.6, f32[32,128]{1,0:T(8,128)} %copy-done.4), custom_call_target="tpu_custom_call" | custom-call | tf_op jit(solution)/shard_map/slotted/pallas_call | solution.py:171
  18.1 31.0 %all_to_all.15 = bf16[32,16,128]{2,1,0:T(8,128)(2,1)S(1)} all-to-all(bf16[32,16,128]{2,1,0:T(8,128)(2,1)} %bitcast.17), channel_id=1, replica_groups=mesh['inp'=2,'chan'=8,'zh'=4,'zl'=2,'x'=4] {'chan','zh'}, dimensions={0} | all-to-all | bytes 262144 | tf_op jit(solution)/shard_map/all_to_all | solution.py:180
  49.1 0.1 broadcast_in_dim.12
  49.2 14.0 %all_to_all.16 = bf16[8,512,128]{2,1,0:T(8,128)(2,1)S(1)} all-to-all(bf16[8,512,128]{2,1,0:T(8,128)(2,1)S(1)} %broadcast_in_dim.12), channel_id=1, replica_groups=mesh['inp'=2,'chan'=8,'zh'=4,'zl'=2,'x'=4] {'zl','x'}, dimensions={0} | all-to-all | bytes 2097152 | tf_op jit(solution)/shard_map/all_to_all | solution.py:184
  63.2 6.9 %collective-permute-start.1 = (bf16[8,512,128]{2,1,0:T(8,128)(2,1)S(1)}, bf16[8,512,128]{2,1,0:T(8,128)(2,1)S(1)}, u32[]{:S(2)}, u32[]{:S(2)}) collective-permute-start(bf16[8,512,128]{2,1,0:T(8,128)(2,1)S(1)} %all_to_all.16), channel_id=1, source_target_pairs={{0,256},{256,0},{1,257},{257,1},{2,258},{258,2},{3,259},{259,3},{4... | collective-permute-start | bytes 3145736 | tf_op jit(solution)/shard_map/ppermute | solution.py:185
  70.2 0.1 pad_add_fusion.place_ref
  70.2 2.2 %collective-permute-done.1 = bf16[8,512,128]{2,1,0:T(8,128)(2,1)S(1)} collective-permute-done((bf16[8,512,128]{2,1,0:T(8,128)(2,1)S(1)}, bf16[8,512,128]{2,1,0:T(8,128)(2,1)S(1)}, u32[]{:S(2)}, u32[]{:S(2)}) %collective-permute-start.1) | collective-permute-done | bytes 1048608 | tf_op jit(solution)/shard_map/ppermute | solution.py:185
  72.4 2.0 %products.1 = bf16[4,64,1088]{2,1,0:T(8,128)(2,1)S(1)} custom-call(s32[2]{0:T(128)S(1)} %pad_add_fusion.place_ref, bf16[8,8,64,128]{3,2,1,0:T(8,128)(2,1)S(1)} %bitcast.12, bf16[8,8,64,128]{3,2,1,0:T(8,128)(2,1)S(1)} %bitcast.13), custom_call_target="tpu_custom_call" | custom-call | tf_op jit(solution)/shard_map/products/pallas_call | solution.py:189
  74.4 19.4 %all_to_all.17 = bf16[4,64,1088]{2,1,0:T(8,128)(2,1)S(1)} all-to-all(bf16[4,64,1088]{2,1,0:T(8,128)(2,1)S(1)} %products.1), channel_id=1, replica_groups=mesh['inp'=2,'chan'=8,'zh'=4,'zl'=2,'x'=4] {'zh'}, dimensions={0} | all-to-all | bytes 1114112 | tf_op jit(solution)/shard_map/all_to_all | solution.py:199
  93.8 1.1 %convert.2 = f32[4,1,2,32,1088]{4,3,2,1,0:T(8,128)} convert(bf16[4,1,2,32,1088]{4,3,2,1,0:T(8,128)(2,1)S(1)} %bitcast.15) | non-fusion elementwise | flops 278528 | bytes 1671168 | tf_op jit(solution)/shard_map/reshape | solution.py:200
Async XLA Ops:
  0.0 2.2 %copy-start = (bf16[128,16384]{1,0:T(8,128)(2,1)S(1)}, bf16[128,16384]{1,0:T(8,128)(2,1)}, u32[]{:S(2)}) copy-start(bf16[128,16384]{1,0:T(8,128)(2,1)} %volts_hbm.1) | copy-start | bytes 12582916
  2.2 1.0 %copy-start.1 = (s32[128,1024]{1,0:T(8,128)S(1)}, s32[128,1024]{1,0:T(8,128)}, u32[]{:S(2)}) copy-start(s32[128,1024]{1,0:T(8,128)} %flags_hbm.1) | copy-start | bytes 1572868
  3.2 0.8 copy-start.3
  4.0 0.7 copy-start.5
  8.8 0.7 copy-start.2
  9.5 0.6 copy-start.4
  10.1 5.6 %collective-permute-start = (f32[6,32,128]{2,1,0:T(8,128)S(1)}, f32[6,32,128]{2,1,0:T(8,128)S(1)}, u32[]{:S(2)}, u32[]{:S(2)}) collective-permute-start(f32[6,32,128]{2,1,0:T(8,128)S(1)} %get-tuple-element.9), channel_id=1, source_target_pairs={{0,1},{1,2},{2,3},{3,4},{4,5},{5,6},{6,7},{7,8},{8,9},{9,10},{10,1... | collective-permute-start | bytes 294920 | tf_op jit(solution)/shard_map/ppermute | solution.py:169
  15.7 0.6 copy-start.6
  63.2 9.2 %collective-permute-start.1 = (bf16[8,512,128]{2,1,0:T(8,128)(2,1)S(1)}, bf16[8,512,128]{2,1,0:T(8,128)(2,1)S(1)}, u32[]{:S(2)}, u32[]{:S(2)}) collective-permute-start(bf16[8,512,128]{2,1,0:T(8,128)(2,1)S(1)} %all_to_all.16), channel_id=1, source_target_pairs={{0,256},{256,0},{1,257},{257,1},{2,258},{258,2},{3,259},{259,3},{4... | collective-permute-start | bytes 3145736 | tf_op jit(solution)/shard_map/ppermute | solution.py:185

commit v2 on v1

v2 whole, which is shorter than its diff:
```python
import math

import jax
import jax.numpy as jnp
import numpy as np
from jax import lax
from jax.experimental import pallas as pl
from jax.experimental.pallas import tpu as pltpu
from jax.sharding import Mesh, PartitionSpec as P

FRAME_SAMPLES = 2048
NCHAN = 1024
TAPS = 4
SLOTS = 32
FRAMES = 8
IN_DEV = 128
LANES = 128
BLK = 32
KT = 34
OWNER_SLOTS = 4
GROUPS = 8
HELD = 5
MESSAGE = 24
SLICE = 72
CARRY = TAPS - 1
SPECTRUM_SCALE = 2.0**-7
NT = (((1,), (1,)), ((), ()))
VMEM = pltpu.VMEM


def window_table():
    sample = np.arange(TAPS * FRAME_SAMPLES, dtype=np.float64)
    middle = (sample + 0.5 - 0.5 * TAPS * FRAME_SAMPLES) / FRAME_SAMPLES
    hanning = 0.5 - 0.5 * np.cos(2.0 * math.pi * (sample + 0.5) / (TAPS * FRAME_SAMPLES))
    return (np.sinc(middle) * hanning).reshape(TAPS, FRAME_SAMPLES).astype(np.float32)


def spectra_kernel(
    slots_hbm, window_hbm, flags_hbm, volts_hbm, out_ref, slots, window, volts, table, flags, rows, sems
):
    small = []
    for index, (source, target) in enumerate(((slots_hbm, slots), (window_hbm, window), (flags_hbm, flags))):
        small.append(pltpu.make_async_copy(source, target, sems.at[FRAMES + index]))
        small[-1].start()
    copies = []
    for frame in range(FRAMES):
        copy = pltpu.make_async_copy(
            volts_hbm.at[:, pl.ds(frame * FRAME_SAMPLES, FRAME_SAMPLES)],
            volts.at[frame // 2, pl.ds(frame % 2 * IN_DEV, IN_DEV), :],
            sems.at[frame],
        )
        copy.start()
        copies.append(copy)

    small[0].wait()
    chosen = lax.broadcasted_iota(jnp.int32, (SLOTS, NCHAN), 0) == slots[...]
    channel = jnp.sum(
        jnp.where(chosen, lax.broadcasted_iota(jnp.int32, (SLOTS, NCHAN), 1), 0).astype(jnp.float32), 1, keepdims=True
    ).astype(jnp.int32)
    lane = lax.broadcasted_iota(jnp.int32, (SLOTS, LANES), 1)
    turn = 2.0 * math.pi / FRAME_SAMPLES
    fine = ((channel * lane) & (FRAME_SAMPLES - 1)).astype(jnp.float32) * turn
    coarse = ((channel * (lane * LANES)) & (FRAME_SAMPLES - 1)).astype(jnp.float32) * turn
    fine_cos, fine_sin = jnp.cos(fine), jnp.sin(fine)
    coarse_cos, coarse_sin = jnp.cos(coarse), jnp.sin(coarse)
    small[1].wait()
    for piece in range(FRAME_SAMPLES // LANES):
        at = pl.ds(piece * LANES, LANES)
        ccos, csin = coarse_cos[:, piece : piece + 1], coarse_sin[:, piece : piece + 1]
        cosine = (ccos * fine_cos - csin * fine_sin).astype(jnp.bfloat16).astype(jnp.float32)
        sine = (-(csin * fine_cos + ccos * fine_sin)).astype(jnp.bfloat16).astype(jnp.float32)
        for tap in range(TAPS):
            weight = window[tap : tap + 1, at]
            table[pl.ds(tap * 64, 32), at] = (cosine * weight).astype(jnp.bfloat16)
            table[pl.ds(tap * 64 + 32, 32), at] = (sine * weight).astype(jnp.bfloat16)

    small[2].wait()
    kept = lax.dot_general(
        chosen.astype(jnp.float32).astype(jnp.bfloat16),
        flags[...].astype(jnp.float32).astype(jnp.bfloat16),
        NT,
        preferred_element_type=jnp.float32,
    )

    sums = {}
    for pair in range(FRAMES // 2):
        copies[2 * pair].wait()
        copies[2 * pair + 1].wait()
        terms = lax.dot_general(table[...], volts[pair], NT, preferred_element_type=jnp.float32)
        for half in range(2):
            for tap in range(TAPS):
                frame = 2 * pair + half + TAPS - 1 - tap
                term = terms[tap * 64 : tap * 64 + 64, half * IN_DEV : (half + 1) * IN_DEV]
                sums[frame] = term if frame not in sums else sums[frame] + term
        for frame in [f for f in sums if f < 2 * pair + 2]:
            done = sums.pop(frame)
            rows[pl.ds(frame, SLOTS, stride=MESSAGE), :] = done[:32] * kept
            rows[pl.ds(FRAMES + frame, SLOTS, stride=MESSAGE), :] = done[32:] * kept
    empty = jnp.zeros((SLOTS, LANES), jnp.float32)
    for frame in range(CARRY + 1):
        real, imag = (sums[FRAMES + frame][:32] * kept, sums[FRAMES + frame][32:] * kept) if frame < CARRY else (empty, empty)
        rows[pl.ds(2 * FRAMES + frame, SLOTS, stride=MESSAGE), :] = real
        rows[pl.ds(2 * FRAMES + 4 + frame, SLOTS, stride=MESSAGE), :] = imag
    out_ref[...] = rows[...].reshape(SLOTS, MESSAGE, LANES).astype(jnp.bfloat16)


def with_carry(real, imag, carried):
    axis = real.ndim - 2
    early = lax.broadcasted_iota(jnp.int32, real.shape, axis) < CARRY
    return real + jnp.where(early, carried, 0.0), imag + jnp.where(early, pltpu.roll(carried, 4, axis), 0.0)


def pack_kernel(in_ref, out_ref):
    slices = []
    for group in range(GROUPS):
        pieces, carried = [], None
        for source in range(4):
            message = in_ref[4 * group + source].astype(jnp.float32)
            real, imag = message[:8], message[8:16]
            if source:
                real, imag = with_carry(real, imag, carried)
            pieces += [real, imag]
            carried = message[16:]
        slices.append(jnp.concatenate(pieces + [carried], 0).astype(jnp.bfloat16))
    for target in range(GROUPS):
        parity = target % 2
        taken = [parity + 2 * i for i in range(4)] + [target + 1 - 2 * parity]
        for place, group in enumerate(taken):
            out_ref[target, place] = slices[group]


def joined(ref, place):
    wide = ref[:, place].astype(jnp.float32)
    carried = jnp.concatenate([jnp.zeros((1, 8, LANES), jnp.float32), wide[: GROUPS - 1, 64:]], 0)
    real, imag = with_carry(wide[:, :8], wide[:, 8:16], carried)
    return jnp.concatenate([real, imag, wide[:, 16:64]], 1).reshape(GROUPS * 64, LANES)


def columns(ref, pair):
    return jnp.concatenate([joined(ref, 2 * pair + i).astype(jnp.bfloat16) for i in range(2)], 1)


def own_kernel(place_ref, own_ref, left_ref, prod_ref):
    same = lax.broadcasted_iota(jnp.int32, (LANES, LANES), 0) == lax.broadcasted_iota(jnp.int32, (LANES, LANES), 1)
    same = same.astype(jnp.float32).astype(jnp.bfloat16)
    depth = GROUPS * 64
    for kind, place in enumerate((place_ref[0], HELD - 1)):
        wide = joined(own_ref, place)
        split = wide.reshape(depth // 16, 16, LANES)
        turned = jnp.concatenate([split[:, 8:], -split[:, :8]], 1).reshape(depth, LANES)
        for half, value in enumerate((wide, turned)):
            left_ref[pl.ds(kind * 256 + half * LANES, LANES), :] = lax.dot_general(
                same, value.astype(jnp.bfloat16), NT, preferred_element_type=jnp.float32
            ).astype(jnp.bfloat16)
    for pair in range(2):
        prod_ref[:, pl.ds(pair * 256, 256)] = jnp.dot(
            left_ref[...], columns(own_ref, pair), preferred_element_type=jnp.float32
        )


def other_kernel(place_ref, left_ref, prod_ref, other_ref, out_ref, ring):
    zh, zl = place_ref[0], place_ref[1]
    ring[:, pl.ds(LANES, 4 * LANES)] = prod_ref[...]
    ring[:, pl.ds(9 * LANES, LANES)] = prod_ref[:, :LANES]
    for pair in range(2):
        value = jnp.dot(left_ref[...], columns(other_ref, pair), preferred_element_type=jnp.float32)
        ring[:, pl.ds((5 + 2 * pair) * LANES, 2 * LANES)] = value
        if pair == 1:
            ring[:, pl.ds(0, LANES)] = value[:, LANES:]
    for kind in range(2):
        target = (zl if kind == 0 else 1 - zl) * 4
        for x in range(4):
            first = zh if kind == 0 else zh - zl + (1 if x else 0)
            start = pl.multiple_of((first + 1) * LANES, LANES)
            for half in range(2):
                row = kind * 256 + half * LANES + x * BLK
                out_ref[target + x, pl.ds(half * BLK, BLK), :] = ring[
                    pl.ds(row, BLK), pl.ds(start, 5 * LANES)
                ].astype(jnp.bfloat16)


def tiles_kernel(place_ref, in_ref, out_ref):
    zl, x, slot = place_ref[1], place_ref[2], pl.program_id(0)
    even = lax.rem(zl + jnp.where(x == 0, 1, 0), 2)
    sides = [in_ref[even * 4 + slot], in_ref[(1 - even) * 4 + slot]]
    pieces = [sides[k % 2][:, k // 2 * LANES : (k // 2 + 1) * LANES] for k in range(10)]
    window = jnp.concatenate(pieces, 1).astype(jnp.float32)
    span = 10 * LANES
    window = pltpu.roll(window, span - lax.rem(x + 3, 4) * BLK, 1)
    out_ref[0] = window[:, : KT * BLK]


def on_device(voltages, input_flags, channel_to_slot):
    hbm = pl.BlockSpec(memory_space=pltpu.HBM)
    vmem = pl.BlockSpec(memory_space=VMEM)
    smem = pl.BlockSpec(memory_space=pltpu.SMEM)
    f32, bf16 = jnp.float32, jnp.bfloat16
    limit = lambda mib: pltpu.CompilerParams(vmem_limit_bytes=mib * 2**20)
    window = jnp.asarray(window_table() * np.float32(SPECTRUM_SCALE))
    place = jnp.stack([lax.axis_index("zh"), lax.axis_index("zl"), lax.axis_index("x")]).astype(jnp.int32)
    slotted = pl.pallas_call(
        spectra_kernel,
        out_shape=jax.ShapeDtypeStruct((SLOTS, MESSAGE, LANES), bf16),
        in_specs=[hbm, hbm, hbm, hbm],
        out_specs=vmem,
        scratch_shapes=[
            VMEM((1, NCHAN), jnp.int32),
            VMEM((TAPS, FRAME_SAMPLES), f32),
            VMEM((FRAMES // 2, 2 * IN_DEV, FRAME_SAMPLES), bf16),
            VMEM((TAPS * 64, FRAME_SAMPLES), bf16),
            VMEM((IN_DEV, NCHAN), jnp.int32),
            VMEM((SLOTS * MESSAGE, LANES), f32),
            pltpu.SemaphoreType.DMA((FRAMES + 3,)),
        ],
        compiler_params=limit(60),
        name="spectra",
    )(channel_to_slot[None, :], window, input_flags, voltages)
    placed = lax.all_to_all(slotted, ("chan", "x"), split_axis=0, concat_axis=0, tiled=True)
    packed = pl.pallas_call(
        pack_kernel,
        out_shape=jax.ShapeDtypeStruct((GROUPS, HELD, SLICE, LANES), bf16),
        in_specs=[vmem],
        out_specs=vmem,
        compiler_params=limit(8),
        name="pack",
    )(placed)
    own = lax.all_to_all(packed, ("zh", "zl"), split_axis=0, concat_axis=0, tiled=True)
    other = lax.ppermute(own, "inp", [(0, 1), (1, 0)])
    depth = GROUPS * 64
    left, prod = pl.pallas_call(
        own_kernel,
        out_shape=(jax.ShapeDtypeStruct((512, depth), bf16), jax.ShapeDtypeStruct((512, 4 * LANES), f32)),
        in_specs=[smem, vmem],
        out_specs=(vmem, vmem),
        compiler_params=limit(8),
        cost_estimate=pl.CostEstimate(flops=2 * 512 * 512 * 512, bytes_accessed=3 * 2**20, transcendentals=0),
        name="own",
    )(place, own)
    rows = pl.pallas_call(
        other_kernel,
        out_shape=jax.ShapeDtypeStruct((8, 64, 5 * LANES), bf16),
        in_specs=[smem, vmem, vmem, vmem],
        out_specs=vmem,
        scratch_shapes=[VMEM((512, 10 * LANES), f32)],
        compiler_params=limit(12),
        name="other",
    )(place, left, prod, other)
    parts = lax.all_to_all(rows, ("zl", "x"), split_axis=0, concat_axis=0, tiled=True)
    tiles = pl.pallas_call(
        tiles_kernel,
        grid=(OWNER_SLOTS,),
        out_shape=jax.ShapeDtypeStruct((OWNER_SLOTS, 64, KT * BLK), f32),
        in_specs=[smem, vmem],
        out_specs=pl.BlockSpec((1, 64, KT * BLK), lambda slot: (slot, 0, 0)),
        compiler_params=limit(8),
        name="tiles",
    )(place, parts)
    return tiles.reshape(OWNER_SLOTS, 1, 2, BLK, KT * BLK)


def solution(mesh):
    parts = Mesh(mesh.devices.reshape(2, 8, 4, 2, 4), ("inp", "chan", "zh", "zl", "x"))
    return jax.shard_map(
        on_device,
        mesh=parts,
        in_specs=(P(("inp", "chan"), ("zh", "zl", "x")), P(("inp", "chan"), None), P()),
        out_specs=P("chan", ("inp", "zh", "zl", "x"), None, None, None),
        check_vma=False,
    )
```

time: 95.4 us -> 79.5 us (0.83)
  local copies, waits for them, and re-layouts: 6.75 us -> 0 us
  starting transfers between devices: 10.8 us -> 6.61 us
  waiting for transfers between devices: 3.8 us -> 0.61 us
  blocking collectives: 64.4 us -> 61.9 us
  Pallas kernels: 7.89 us -> 10 us
  other arithmetic: 1.18 us -> 0.08 us
    unnamed x14 -> x0, local copies, waits for them, and re-layouts: 6.62 us -> none
    ppermute x1 -> x0, starting transfers between devices: 3.94 us -> none  [on_device(): history = lax.ppermute(part, ('zh', 'zl', 'x'), groups)]
    all_to_all x3, blocking collectives: 64.4 us -> 61.9 us  [the longest x1 28.1 us: on_device(): lax.all_to_all(packed, ('zh', 'zl'), split_axis=0, concat_axis=0, tiled=T...]
    pallas_call x3 -> x5, Pallas kernels: 7.89 us -> 10 us  [the longest x1 5.23 us: on_device(): pl.pallas_call(spectra_kernel, out_shape=jax.ShapeDtypeStruct((SLOTS, MES...]
    ppermute x1 -> x0, waiting for transfers between devices: 1.62 us -> none  [on_device(): history = lax.ppermute(part, ('zh', 'zl', 'x'), groups)]
    ppermute x1, waiting for transfers between devices: 2.18 us -> 0.61 us  [on_device(): other = lax.ppermute(own, 'inp', [(0, 1), (1, 0)])]
    reshape x1 -> x0, other arithmetic: 1.1 us -> none  [on_device(): return tiles.astype(f32).reshape(ROW_TARGETS, 1, 2, BLK, KT * BLK)]
  transfers between devices with their start and end apart: 2 -> 1, of which waited for: 2 -> 1; matrix products, arithmetic and copies ran while one was open for 0% -> 0% of each run, Pallas kernels for 0% -> 1%
where the time goes in v2:
time: 79.5 us; the launch traced here: 79.2 us
  blocking collectives  61.9 us (78%)
  Pallas kernels  10 us (13%)
  starting transfers between devices  6.61 us (8%)
    all_to_all x1, blocking collectives, on_device(): lax.all_to_all(packed, ('zh', 'zl'), split_axis=0, concat_axis=0, tiled=T...  28.1 us
    all_to_all x1, blocking collectives, on_device(): lax.all_to_all(slotted, ('chan', 'x'), split_axis=0, concat_axis=0, tiled...  20.4 us
    all_to_all x1, blocking collectives, on_device(): lax.all_to_all(rows, ('zl', 'x'), split_axis=0, concat_axis=0, tiled=True)  13.3 us
    ppermute x1, starting transfers between devices, on_device(): other = lax.ppermute(own, 'inp', [(0, 1), (1, 0)])  6.61 us
    pallas_call x1, Pallas kernels, on_device(): pl.pallas_call(spectra_kernel, out_shape=jax.ShapeDtypeStruct((SLOTS, MES...  5.23 us
    pallas_call x1, Pallas kernels, on_device(): pl.pallas_call(tiles_kernel, grid=(OWNER_SLOTS,), out_shape=jax.ShapeDtyp...  2.48 us
  transfers between devices with their start and end apart: 1, of which 1 were waited for; matrix products, arithmetic and copies ran while one was open for 0% of the time, Pallas kernels for 1%

profile of v2, /device:TPU:1, one launch (start us, length us, event | category | flops | bytes accessed | tf_op | source)
XLA Modules:
  0.0 79.2 jit_solution(17228023790474078478)
XLA Ops:
  0.0 5.2 %spectra.1 = bf16[32,24,128]{2,1,0:T(8,128)(2,1)} custom-call(s32[1,1024]{1,0:T(1,128)} %bitcast.7, f32[4,2048]{1,0:T(4,128)} %constant.14.clone.window_hbm, s32[128,1024]{1,0:T(8,128)} %flags_hbm.1, bf16[128,16384]{1,0:T(8,128)(2,1)} %volts_hbm.1), custom_call_target="tpu_custom_call" | custom-call | tf_op jit(solution)/shard_map/spectra/pallas_call | solution.py:201
  5.2 20.4 %all_to_all.15.in_ref = bf16[32,24,128]{2,1,0:T(8,128)(2,1)S(1)} all-to-all(bf16[32,24,128]{2,1,0:T(8,128)(2,1)} %spectra.1), channel_id=1, replica_groups=mesh['inp'=2,'chan'=8,'zh'=4,'zl'=2,'x'=4] {'chan','x'}, dimensions={0} | all-to-all | bytes 393216 | tf_op jit(solution)/shard_map/all_to_all | solution.py:218
  25.7 0.1 pack.1
  25.7 28.1 %all_to_all.16.own_ref = bf16[8,5,72,128]{3,2,1,0:T(8,128)(2,1)S(1)} all-to-all(bf16[8,5,72,128]{3,2,1,0:T(8,128)(2,1)S(1)} %pack.1), channel_id=1, replica_groups=mesh['inp'=2,'chan'=8,'zh'=4,'zl'=2,'x'=4] {'zh','zl'}, dimensions={0} | all-to-all | bytes 1474560 | tf_op jit(solution)/shard_map/all_to_all | solution.py:227
  53.9 6.6 %collective-permute-start = (bf16[8,5,72,128]{3,2,1,0:T(8,128)(2,1)S(1)}, bf16[8,5,72,128]{3,2,1,0:T(8,128)(2,1)S(1)}, u32[]{:S(2)}, u32[]{:S(2)}) collective-permute-start(bf16[8,5,72,128]{3,2,1,0:T(8,128)(2,1)S(1)} %all_to_all.16.own_ref), channel_id=1, source_target_pairs={{0,256},{256,0},{1,257},{257,1},{2,258},{258,2},{3,259},{259,3},{4... | collective-permute-start | bytes 2211848 | tf_op jit(solution)/shard_map/ppermute | solution.py:228
  60.5 0.1 pad_add_fusion.place_ref
  60.6 1.1 %own.1 = (bf16[512,512]{1,0:T(8,128)(2,1)S(1)}, f32[512,512]{1,0:T(8,128)S(1)}) custom-call(s32[3]{0:T(128)S(1)} %pad_add_fusion.place_ref, bf16[8,5,72,128]{3,2,1,0:T(8,128)(2,1)S(1)} %all_to_all.16.own_ref), custom_call_target="tpu_custom_call" | custom-call | flops 268435456 | bytes 3145728 | tf_op jit(solution)/shard_map/own/pallas_call | solution.py:230
  61.7 0.6 collective-permute-done.other_ref
  62.3 1.1 %other.1 = bf16[8,64,640]{2,1,0:T(8,128)(2,1)S(1)} custom-call(s32[3]{0:T(128)S(1)} %pad_add_fusion.place_ref, bf16[512,512]{1,0:T(8,128)(2,1)S(1)} %get-tuple-element.7.left_ref, f32[512,512]{1,0:T(8,128)S(1)} %get-tuple-element.8.prod_ref, bf16[8,5,72,128]{3,2,1,0:T(8,128)(2,1)S(1)} %collective-permute-done.other_ref), custom_call_target="tpu_custom_call" | custom-call | tf_op jit(solution)/shard_map/other/pallas_call | solution.py:239
  63.5 13.3 %all_to_all.17.in_ref = bf16[8,64,640]{2,1,0:T(8,128)(2,1)S(1)} all-to-all(bf16[8,64,640]{2,1,0:T(8,128)(2,1)S(1)} %other.1), channel_id=1, replica_groups=mesh['inp'=2,'chan'=8,'zh'=4,'zl'=2,'x'=4] {'zl','x'}, dimensions={0} | all-to-all | bytes 1310720 | tf_op jit(solution)/shard_map/all_to_all | solution.py:248
  76.7 2.5 %tiles.1 = f32[4,64,1088]{2,1,0:T(8,128)} custom-call(s32[3]{0:T(128)S(1)} %pad_add_fusion.place_ref, bf16[8,64,640]{2,1,0:T(8,128)(2,1)S(1)} %all_to_all.17.in_ref), custom_call_target="tpu_custom_call" | custom-call | tf_op jit(solution)/shard_map/tiles/pallas_call | solution.py:249
Async XLA Ops:
  53.9 8.4 %collective-permute-start = (bf16[8,5,72,128]{3,2,1,0:T(8,128)(2,1)S(1)}, bf16[8,5,72,128]{3,2,1,0:T(8,128)(2,1)S(1)}, u32[]{:S(2)}, u32[]{:S(2)}) collective-permute-start(bf16[8,5,72,128]{3,2,1,0:T(8,128)(2,1)S(1)} %all_to_all.16.own_ref), channel_id=1, source_target_pairs={{0,256},{256,0},{1,257},{257,1},{2,258},{258,2},{3,259},{259,3},{4... | collective-permute-start | bytes 2211848 | tf_op jit(solution)/shard_map/ppermute | solution.py:228

commit v3 on v2

--- a/solution.py
+++ b/solution.py
@@ -84,8 +84,9 @@
 
     sums = {}
     for pair in range(FRAMES // 2):
-        copies[2 * pair].wait()
-        copies[2 * pair + 1].wait()
+        if pair % 2 == 0:
+            for copy in copies[2 * pair : 2 * pair + 4]:
+                copy.wait()
         terms = lax.dot_general(table[...], volts[pair], NT, preferred_element_type=jnp.float32)
         for half in range(2):
             for tap in range(TAPS):
@@ -140,11 +141,11 @@
     return jnp.concatenate([joined(ref, 2 * pair + i).astype(jnp.bfloat16) for i in range(2)], 1)
 
 
-def own_kernel(place_ref, own_ref, left_ref, prod_ref):
+def own_kernel(own_ref, left_ref, prod_ref):
     same = lax.broadcasted_iota(jnp.int32, (LANES, LANES), 0) == lax.broadcasted_iota(jnp.int32, (LANES, LANES), 1)
     same = same.astype(jnp.float32).astype(jnp.bfloat16)
     depth = GROUPS * 64
-    for kind, place in enumerate((place_ref[0], HELD - 1)):
+    for kind, place in enumerate((lax.axis_index("zh"), HELD - 1)):
         wide = joined(own_ref, place)
         split = wide.reshape(depth // 16, 16, LANES)
         turned = jnp.concatenate([split[:, 8:], -split[:, :8]], 1).reshape(depth, LANES)
@@ -158,8 +159,8 @@
         )
 
 
-def other_kernel(place_ref, left_ref, prod_ref, other_ref, out_ref, ring):
-    zh, zl = place_ref[0], place_ref[1]
+def other_kernel(left_ref, prod_ref, other_ref, out_ref, ring):
+    zh, zl = lax.axis_index("zh"), lax.axis_index("zl")
     ring[:, pl.ds(LANES, 4 * LANES)] = prod_ref[...]
     ring[:, pl.ds(9 * LANES, LANES)] = prod_ref[:, :LANES]
     for pair in range(2):
@@ -179,28 +180,33 @@
                 ].astype(jnp.bfloat16)
 
 
-def tiles_kernel(place_ref, in_ref, out_ref):
-    zl, x, slot = place_ref[1], place_ref[2], pl.program_id(0)
+def tiles_kernel(in_ref, out_hbm, tiles, sems):
+    zl, x = lax.axis_index("zl"), lax.axis_index("x")
     even = lax.rem(zl + jnp.where(x == 0, 1, 0), 2)
-    sides = [in_ref[even * 4 + slot], in_ref[(1 - even) * 4 + slot]]
-    pieces = [sides[k % 2][:, k // 2 * LANES : (k // 2 + 1) * LANES] for k in range(10)]
-    window = jnp.concatenate(pieces, 1).astype(jnp.float32)
     span = 10 * LANES
-    window = pltpu.roll(window, span - lax.rem(x + 3, 4) * BLK, 1)
-    out_ref[0] = window[:, : KT * BLK]
+    shift = span - lax.rem(x + 3, 4) * BLK
+    copies = []
+    for slot in range(OWNER_SLOTS):
+        sides = [in_ref[even * 4 + slot], in_ref[(1 - even) * 4 + slot]]
+        pieces = [sides[k % 2][:, k // 2 * LANES : (k // 2 + 1) * LANES] for k in range(10)]
+        window = pltpu.roll(jnp.concatenate(pieces, 1).astype(jnp.float32), shift, 1)
+        tiles[slot] = window[:, : KT * BLK]
+        copies.append(pltpu.make_async_copy(tiles.at[slot], out_hbm.at[slot], sems.at[slot]))
+        copies[-1].start()
+    for copy in copies:
+        copy.wait()
 
 
 def on_device(voltages, input_flags, channel_to_slot):
     hbm = pl.BlockSpec(memory_space=pltpu.HBM)
     vmem = pl.BlockSpec(memory_space=VMEM)
-    smem = pl.BlockSpec(memory_space=pltpu.SMEM)
     f32, bf16 = jnp.float32, jnp.bfloat16
     limit = lambda mib: pltpu.CompilerParams(vmem_limit_bytes=mib * 2**20)
+    in_hbm = lambda value: pltpu.with_memory_space_constraint(value, pltpu.HBM)
     window = jnp.asarray(window_table() * np.float32(SPECTRUM_SCALE))
-    place = jnp.stack([lax.axis_index("zh"), lax.axis_index("zl"), lax.axis_index("x")]).astype(jnp.int32)
     slotted = pl.pallas_call(
         spectra_kernel,
-        out_shape=jax.ShapeDtypeStruct((SLOTS, MESSAGE, LANES), bf16),
+        out_shape=VMEM((SLOTS, MESSAGE, LANES), bf16),
         in_specs=[hbm, hbm, hbm, hbm],
         out_specs=vmem,
         scratch_shapes=[
@@ -212,9 +218,9 @@
             VMEM((SLOTS * MESSAGE, LANES), f32),
             pltpu.SemaphoreType.DMA((FRAMES + 3,)),
         ],
-        compiler_params=limit(60),
+        compiler_params=limit(16),
         name="spectra",
-    )(channel_to_slot[None, :], window, input_flags, voltages)
+    )(*(in_hbm(value) for value in (channel_to_slot[None, :], window, input_flags, voltages)))
     placed = lax.all_to_all(slotted, ("chan", "x"), split_axis=0, concat_axis=0, tiled=True)
     packed = pl.pallas_call(
         pack_kernel,
@@ -230,31 +236,31 @@
     left, prod = pl.pallas_call(
         own_kernel,
         out_shape=(jax.ShapeDtypeStruct((512, depth), bf16), jax.ShapeDtypeStruct((512, 4 * LANES), f32)),
-        in_specs=[smem, vmem],
+        in_specs=[vmem],
         out_specs=(vmem, vmem),
         compiler_params=limit(8),
         cost_estimate=pl.CostEstimate(flops=2 * 512 * 512 * 512, bytes_accessed=3 * 2**20, transcendentals=0),
         name="own",
-    )(place, own)
+    )(own)
     rows = pl.pallas_call(
         other_kernel,
         out_shape=jax.ShapeDtypeStruct((8, 64, 5 * LANES), bf16),
-        in_specs=[smem, vmem, vmem, vmem],
+        in_specs=[vmem, vmem, vmem],
         out_specs=vmem,
         scratch_shapes=[VMEM((512, 10 * LANES), f32)],
         compiler_params=limit(12),
         name="other",
-    )(place, left, prod, other)
+    )(left, prod, other)
     parts = lax.all_to_all(rows, ("zl", "x"), split_axis=0, concat_axis=0, tiled=True)
     tiles = pl.pallas_call(
         tiles_kernel,
-        grid=(OWNER_SLOTS,),
         out_shape=jax.ShapeDtypeStruct((OWNER_SLOTS, 64, KT * BLK), f32),
-        in_specs=[smem, vmem],
-        out_specs=pl.BlockSpec((1, 64, KT * BLK), lambda slot: (slot, 0, 0)),
+        in_specs=[vmem],
+        out_specs=hbm,
+        scratch_shapes=[VMEM((OWNER_SLOTS, 64, KT * BLK), f32), pltpu.SemaphoreType.DMA((OWNER_SLOTS,))],
         compiler_params=limit(8),
         name="tiles",
-    )(place, parts)
+    )(parts)
     return tiles.reshape(OWNER_SLOTS, 1, 2, BLK, KT * BLK)
 
 

time: 79.5 us -> 75.6 us (0.951)
  Pallas kernels: 10 us -> 5.8 us
    pallas_call x2, Pallas kernels: 7.71 us -> 4.59 us  [the longest x1 3.39 us: on_device(): pl.pallas_call(spectra_kernel, out_shape=VMEM((SLOTS, MESSAGE, LANES), bf...]
where the time goes in v3:
time: 75.6 us; the launch traced here: 75.4 us
  blocking collectives  61.7 us (82%)
  starting transfers between devices  6.62 us (9%)
  Pallas kernels  5.8 us (8%)
  waiting for transfers between devices  1.22 us (2%)
    all_to_all x1, blocking collectives, on_device(): lax.all_to_all(packed, ('zh', 'zl'), split_axis=0, concat_axis=0, tiled=T...  28.1 us
    all_to_all x1, blocking collectives, on_device(): lax.all_to_all(slotted, ('chan', 'x'), split_axis=0, concat_axis=0, tiled...  20.2 us
    all_to_all x1, blocking collectives, on_device(): lax.all_to_all(rows, ('zl', 'x'), split_axis=0, concat_axis=0, tiled=True)  13.3 us
    ppermute x1, starting transfers between devices, on_device(): other = lax.ppermute(own, 'inp', [(0, 1), (1, 0)])  6.62 us
    pallas_call x1, Pallas kernels, on_device(): pl.pallas_call(spectra_kernel, out_shape=VMEM((SLOTS, MESSAGE, LANES), bf...  3.39 us
  transfers between devices with their start and end apart: 1, of which 1 were waited for; matrix products, arithmetic and copies ran while one was open for 0% of the time, Pallas kernels for 1%

profile of v3, /device:TPU:1, one launch (start us, length us, event | category | flops | bytes accessed | tf_op | source)
XLA Modules:
  0.0 75.4 jit_solution(17357228036240898032)
XLA Ops:
  0.0 3.4 %spectra.1 = bf16[32,24,128]{2,1,0:T(8,128)(2,1)S(1)} custom-call(s32[1,1024]{1,0:T(1,128)} %bitcast.4, f32[4,2048]{1,0:T(4,128)} %constant.2.clone.window_hbm, s32[128,1024]{1,0:T(8,128)} %flags_hbm.1, bf16[128,16384]{1,0:T(8,128)(2,1)} %volts_hbm.1), custom_call_target="tpu_custom_call" | custom-call | tf_op jit(solution)/shard_map/spectra/pallas_call | solution.py:207
  3.4 20.2 %all_to_all.15.in_ref = bf16[32,24,128]{2,1,0:T(8,128)(2,1)S(1)} all-to-all(bf16[32,24,128]{2,1,0:T(8,128)(2,1)S(1)} %spectra.1), channel_id=1, replica_groups=mesh['inp'=2,'chan'=8,'zh'=4,'zl'=2,'x'=4] {'chan','x'}, dimensions={0} | all-to-all | bytes 393216 | tf_op jit(solution)/shard_map/all_to_all | solution.py:224
  23.6 0.1 pack.1
  23.7 28.1 %all_to_all.16.own_ref = bf16[8,5,72,128]{3,2,1,0:T(8,128)(2,1)S(1)} all-to-all(bf16[8,5,72,128]{3,2,1,0:T(8,128)(2,1)S(1)} %pack.1), channel_id=1, replica_groups=mesh['inp'=2,'chan'=8,'zh'=4,'zl'=2,'x'=4] {'zh','zl'}, dimensions={0} | all-to-all | bytes 1474560 | tf_op jit(solution)/shard_map/all_to_all | solution.py:233
  51.8 6.6 %collective-permute-start = (bf16[8,5,72,128]{3,2,1,0:T(8,128)(2,1)S(1)}, bf16[8,5,72,128]{3,2,1,0:T(8,128)(2,1)S(1)}, u32[]{:S(2)}, u32[]{:S(2)}) collective-permute-start(bf16[8,5,72,128]{3,2,1,0:T(8,128)(2,1)S(1)} %all_to_all.16.own_ref), channel_id=1, source_target_pairs={{0,256},{256,0},{1,257},{257,1},{2,258},{258,2},{3,259},{259,3},{4... | collective-permute-start | bytes 2211848 | tf_op jit(solution)/shard_map/ppermute | solution.py:234
  58.5 0.6 own.1
  59.1 1.2 %collective-permute-done.other_ref = bf16[8,5,72,128]{3,2,1,0:T(8,128)(2,1)S(1)} collective-permute-done((bf16[8,5,72,128]{3,2,1,0:T(8,128)(2,1)S(1)}, bf16[8,5,72,128]{3,2,1,0:T(8,128)(2,1)S(1)}, u32[]{:S(2)}, u32[]{:S(2)}) %collective-permute-start) | collective-permute-done | bytes 737312 | tf_op jit(solution)/shard_map/ppermute | solution.py:234
  60.3 0.5 other.1
  60.8 13.3 %all_to_all.17.in_ref = bf16[8,64,640]{2,1,0:T(8,128)(2,1)S(1)} all-to-all(bf16[8,64,640]{2,1,0:T(8,128)(2,1)S(1)} %other.1), channel_id=1, replica_groups=mesh['inp'=2,'chan'=8,'zh'=4,'zl'=2,'x'=4] {'zl','x'}, dimensions={0} | all-to-all | bytes 1310720 | tf_op jit(solution)/shard_map/all_to_all | solution.py:254
  74.2 1.2 %tiles.1 = f32[4,64,1088]{2,1,0:T(8,128)} custom-call(bf16[8,64,640]{2,1,0:T(8,128)(2,1)S(1)} %all_to_all.17.in_ref), custom_call_target="tpu_custom_call" | custom-call | tf_op jit(solution)/shard_map/tiles/pallas_call | solution.py:255
Async XLA Ops:
  51.8 8.4 %collective-permute-start = (bf16[8,5,72,128]{3,2,1,0:T(8,128)(2,1)S(1)}, bf16[8,5,72,128]{3,2,1,0:T(8,128)(2,1)S(1)}, u32[]{:S(2)}, u32[]{:S(2)}) collective-permute-start(bf16[8,5,72,128]{3,2,1,0:T(8,128)(2,1)S(1)} %all_to_all.16.own_ref), channel_id=1, source_target_pairs={{0,256},{256,0},{1,257},{257,1},{2,258},{258,2},{3,259},{259,3},{4... | collective-permute-start | bytes 2211848 | tf_op jit(solution)/shard_map/ppermute | solution.py:234

commit v4 on v3

--- a/solution.py
+++ b/solution.py
@@ -21,7 +21,10 @@
 GROUPS = 8
 HELD = 5
 MESSAGE = 24
-SLICE = 72
+SLICE = 64
+BUNDLE = HELD * SLICE + 32
+CUT = 18 * BLK
+PARCEL = 4 * 64 + 32
 CARRY = TAPS - 1
 SPECTRUM_SCALE = 2.0**-7
 NT = (((1,), (1,)), ((), ()))
@@ -112,7 +115,7 @@
 
 
 def pack_kernel(in_ref, out_ref):
-    slices = []
+    slices, sums = [], []
     for group in range(GROUPS):
         pieces, carried = [], None
         for source in range(4):
@@ -122,19 +125,37 @@
                 real, imag = with_carry(real, imag, carried)
             pieces += [real, imag]
             carried = message[16:]
-        slices.append(jnp.concatenate(pieces + [carried], 0).astype(jnp.bfloat16))
+        slices.append(jnp.concatenate(pieces, 0).astype(jnp.bfloat16))
+        sums.append(carried)
+    unused = lax.broadcasted_iota(jnp.int32, (8, LANES), 0) % 4 == CARRY
     for target in range(GROUPS):
         parity = target % 2
-        taken = [parity + 2 * i for i in range(4)] + [target + 1 - 2 * parity]
-        for place, group in enumerate(taken):
-            out_ref[target, place] = slices[group]
+        extra = target + 1 - 2 * parity
+        taken = [parity + 2 * i for i in range(4)]
+        for place, group in enumerate(taken + [extra]):
+            out_ref[target, pl.ds(place * SLICE, SLICE), :] = slices[group]
+        last = [
+            jnp.where(unused, pltpu.roll(sums[extra], CARRY - i, 0), sums[group]) if i < CARRY else sums[group]
+            for i, group in enumerate(taken)
+        ]
+        out_ref[target, pl.ds(HELD * SLICE, 32), :] = jnp.concatenate(last, 0).astype(jnp.bfloat16)
 
 
 def joined(ref, place):
-    wide = ref[:, place].astype(jnp.float32)
-    carried = jnp.concatenate([jnp.zeros((1, 8, LANES), jnp.float32), wide[: GROUPS - 1, 64:]], 0)
+    start = place * SLICE if isinstance(place, int) else pl.multiple_of(place * SLICE, SLICE)
+    wide = ref[:, pl.ds(start, SLICE), :].astype(jnp.float32)
+    sums = ref[: GROUPS - 1, pl.ds(HELD * SLICE, 32), :].astype(jnp.float32)
+    sums = [sums[:, 8 * i : 8 * i + 8] for i in range(4)]
+    if not isinstance(place, int):
+        carried = sum(jnp.where(place == i, sums[i], 0.0) for i in range(4))
+    elif place < 4:
+        carried = sums[place]
+    else:
+        row = lax.broadcasted_iota(jnp.int32, sums[0].shape, 1) % 4
+        carried = sum(jnp.where(row == i, pltpu.roll(sums[i], 5 + i, 1), 0.0) for i in range(CARRY))
+    carried = jnp.concatenate([jnp.zeros((1, 8, LANES), jnp.float32), carried], 0)
     real, imag = with_carry(wide[:, :8], wide[:, 8:16], carried)
-    return jnp.concatenate([real, imag, wide[:, 16:64]], 1).reshape(GROUPS * 64, LANES)
+    return jnp.concatenate([real, imag, wide[:, 16:]], 1).reshape(GROUPS * SLICE, LANES)
 
 
 def columns(ref, pair):
@@ -168,29 +189,46 @@
         ring[:, pl.ds((5 + 2 * pair) * LANES, 2 * LANES)] = value
         if pair == 1:
             ring[:, pl.ds(0, LANES)] = value[:, LANES:]
+    lane = lax.broadcasted_iota(jnp.int32, (BLK, LANES), 1)
     for kind in range(2):
         target = (zl if kind == 0 else 1 - zl) * 4
         for x in range(4):
             first = zh if kind == 0 else zh - zl + (1 if x else 0)
             start = pl.multiple_of((first + 1) * LANES, LANES)
+            skipped = (x + 3) % 4 * BLK
+            leads = (kind == 0) == (x > 0)
+            lasts = []
             for half in range(2):
-                row = kind * 256 + half * LANES + x * BLK
-                out_ref[target + x, pl.ds(half * BLK, BLK), :] = ring[
-                    pl.ds(row, BLK), pl.ds(start, 5 * LANES)
-                ].astype(jnp.bfloat16)
+                value = ring[pl.ds(kind * 256 + half * LANES + x * BLK, BLK), pl.ds(start, 5 * LANES)]
+                groups = [value[:, i * LANES : (i + 1) * LANES] for i in range(5)]
+                if skipped:
+                    groups = [pltpu.roll(group, LANES - skipped, 1) for group in groups]
+                lasts.append(groups[4][:, : LANES // 2])
+                if leads and skipped:
+                    groups[0] = jnp.where(lane < LANES - skipped, groups[0], groups[4])
+                for tile in range(4):
+                    out_ref[target + x, pl.ds(tile * 64 + half * BLK, BLK), :] = groups[tile].astype(jnp.bfloat16)
+            out_ref[target + x, pl.ds(256, BLK), :] = jnp.concatenate(lasts, 1).astype(jnp.bfloat16)
 
 
 def tiles_kernel(in_ref, out_hbm, tiles, sems):
     zl, x = lax.axis_index("zl"), lax.axis_index("x")
-    even = lax.rem(zl + jnp.where(x == 0, 1, 0), 2)
-    span = 10 * LANES
-    shift = span - lax.rem(x + 3, 4) * BLK
+    leading = lax.rem(zl + jnp.where(x == 0, 1, 0), 2)
+    first = lax.broadcasted_iota(jnp.int32, (64, LANES), 1) < LANES - lax.rem(x + 3, 4) * BLK
     copies = []
     for slot in range(OWNER_SLOTS):
-        sides = [in_ref[even * 4 + slot], in_ref[(1 - even) * 4 + slot]]
-        pieces = [sides[k % 2][:, k // 2 * LANES : (k // 2 + 1) * LANES] for k in range(10)]
-        window = pltpu.roll(jnp.concatenate(pieces, 1).astype(jnp.float32), shift, 1)
-        tiles[slot] = window[:, : KT * BLK]
+        sides = []
+        for parity in (leading, 1 - leading):
+            wide = in_ref[parity * 4 + slot].astype(jnp.float32)
+            last = wide[256:]
+            sides.append([wide[64 * i : 64 * i + 64] for i in range(4)] + [
+                jnp.concatenate([last, pltpu.roll(last, LANES // 2, 1)], 0)
+            ])
+        even, odd = sides
+        for i in range(4):
+            tiles[slot, :, pl.ds(2 * i * LANES, LANES)] = jnp.where(first, even[i], odd[i])
+            tiles[slot, :, pl.ds((2 * i + 1) * LANES, LANES)] = jnp.where(first, odd[i], even[(i + 1) % 4])
+        tiles[slot, :, pl.ds(8 * LANES, LANES // 2)] = jnp.where(first, even[4], odd[4])[:, : LANES // 2]
         copies.append(pltpu.make_async_copy(tiles.at[slot], out_hbm.at[slot], sems.at[slot]))
         copies[-1].start()
     for copy in copies:
@@ -224,7 +262,7 @@
     placed = lax.all_to_all(slotted, ("chan", "x"), split_axis=0, concat_axis=0, tiled=True)
     packed = pl.pallas_call(
         pack_kernel,
-        out_shape=jax.ShapeDtypeStruct((GROUPS, HELD, SLICE, LANES), bf16),
+        out_shape=jax.ShapeDtypeStruct((GROUPS, BUNDLE, LANES), bf16),
         in_specs=[vmem],
         out_specs=vmem,
         compiler_params=limit(8),
@@ -244,7 +282,7 @@
     )(own)
     rows = pl.pallas_call(
         other_kernel,
-        out_shape=jax.ShapeDtypeStruct((8, 64, 5 * LANES), bf16),
+        out_shape=jax.ShapeDtypeStruct((8, PARCEL, LANES), bf16),
         in_specs=[vmem, vmem, vmem],
         out_specs=vmem,
         scratch_shapes=[VMEM((512, 10 * LANES), f32)],

time: 75.6 us -> 74.9 us (level)
  blocking collectives: 61.7 us -> 60.9 us
where the time goes in v4:
time: 74.9 us; the launch traced here: 74.7 us
  blocking collectives  60.9 us (81%)
  starting transfers between devices  6.59 us (9%)
  Pallas kernels  5.93 us (8%)
  waiting for transfers between devices  1.2 us (2%)
    all_to_all x1, blocking collectives, on_device(): lax.all_to_all(packed, ('zh', 'zl'), split_axis=0, concat_axis=0, tiled=T...  27.8 us
    all_to_all x1, blocking collectives, on_device(): lax.all_to_all(slotted, ('chan', 'x'), split_axis=0, concat_axis=0, tiled...  20.2 us
    all_to_all x1, blocking collectives, on_device(): lax.all_to_all(rows, ('zl', 'x'), split_axis=0, concat_axis=0, tiled=True)  12.9 us
    ppermute x1, starting transfers between devices, on_device(): other = lax.ppermute(own, 'inp', [(0, 1), (1, 0)])  6.59 us
    pallas_call x1, Pallas kernels, on_device(): pl.pallas_call(spectra_kernel, out_shape=VMEM((SLOTS, MESSAGE, LANES), bf...  3.39 us
  transfers between devices with their start and end apart: 1, of which 1 were waited for; matrix products, arithmetic and copies ran while one was open for 0% of the time, Pallas kernels for 1%

profile of v4, /device:TPU:1, one launch (start us, length us, event | category | flops | bytes accessed | tf_op | source)
XLA Modules:
  0.0 74.7 jit_solution(3555725367888422529)
XLA Ops:
  0.0 3.4 %spectra.1 = bf16[32,24,128]{2,1,0:T(8,128)(2,1)S(1)} custom-call(s32[1,1024]{1,0:T(1,128)} %bitcast.4, f32[4,2048]{1,0:T(4,128)} %constant.2.clone.window_hbm, s32[128,1024]{1,0:T(8,128)} %flags_hbm.1, bf16[128,16384]{1,0:T(8,128)(2,1)} %volts_hbm.1), custom_call_target="tpu_custom_call" | custom-call | tf_op jit(solution)/shard_map/spectra/pallas_call | solution.py:245
  3.4 20.2 %all_to_all.15.in_ref = bf16[32,24,128]{2,1,0:T(8,128)(2,1)S(1)} all-to-all(bf16[32,24,128]{2,1,0:T(8,128)(2,1)S(1)} %spectra.1), channel_id=1, replica_groups=mesh['inp'=2,'chan'=8,'zh'=4,'zl'=2,'x'=4] {'chan','x'}, dimensions={0} | all-to-all | bytes 393216 | tf_op jit(solution)/shard_map/all_to_all | solution.py:262
  23.6 0.1 pack.1
  23.7 27.8 %all_to_all.16.own_ref = bf16[8,352,128]{2,1,0:T(8,128)(2,1)S(1)} all-to-all(bf16[8,352,128]{2,1,0:T(8,128)(2,1)S(1)} %pack.1), channel_id=1, replica_groups=mesh['inp'=2,'chan'=8,'zh'=4,'zl'=2,'x'=4] {'zh','zl'}, dimensions={0} | all-to-all | bytes 1441792 | tf_op jit(solution)/shard_map/all_to_all | solution.py:271
  51.5 6.6 %collective-permute-start = (bf16[8,352,128]{2,1,0:T(8,128)(2,1)S(1)}, bf16[8,352,128]{2,1,0:T(8,128)(2,1)S(1)}, u32[]{:S(2)}, u32[]{:S(2)}) collective-permute-start(bf16[8,352,128]{2,1,0:T(8,128)(2,1)S(1)} %all_to_all.16.own_ref), channel_id=1, source_target_pairs={{0,256},{256,0},{1,257},{257,1},{2,258},{258,2},{3,259},{259,3},{4... | collective-permute-start | bytes 2162696 | tf_op jit(solution)/shard_map/ppermute | solution.py:272
  58.1 0.6 own.1
  58.7 1.2 %collective-permute-done.other_ref = bf16[8,352,128]{2,1,0:T(8,128)(2,1)S(1)} collective-permute-done((bf16[8,352,128]{2,1,0:T(8,128)(2,1)S(1)}, bf16[8,352,128]{2,1,0:T(8,128)(2,1)S(1)}, u32[]{:S(2)}, u32[]{:S(2)}) %collective-permute-start) | collective-permute-done | bytes 720928 | tf_op jit(solution)/shard_map/ppermute | solution.py:272
  59.9 0.7 other.1
  60.6 12.9 %all_to_all.17.in_ref = bf16[8,288,128]{2,1,0:T(8,128)(2,1)S(1)} all-to-all(bf16[8,288,128]{2,1,0:T(8,128)(2,1)S(1)} %other.1), channel_id=1, replica_groups=mesh['inp'=2,'chan'=8,'zh'=4,'zl'=2,'x'=4] {'zl','x'}, dimensions={0} | all-to-all | bytes 1179648 | tf_op jit(solution)/shard_map/all_to_all | solution.py:292
  73.5 1.1 %tiles.1 = f32[4,64,1088]{2,1,0:T(8,128)} custom-call(bf16[8,288,128]{2,1,0:T(8,128)(2,1)S(1)} %all_to_all.17.in_ref), custom_call_target="tpu_custom_call" | custom-call | tf_op jit(solution)/shard_map/tiles/pallas_call | solution.py:293
Async XLA Ops:
  51.5 8.4 %collective-permute-start = (bf16[8,352,128]{2,1,0:T(8,128)(2,1)S(1)}, bf16[8,352,128]{2,1,0:T(8,128)(2,1)S(1)}, u32[]{:S(2)}, u32[]{:S(2)}) collective-permute-start(bf16[8,352,128]{2,1,0:T(8,128)(2,1)S(1)} %all_to_all.16.own_ref), channel_id=1, source_target_pairs={{0,256},{256,0},{1,257},{257,1},{2,258},{258,2},{3,259},{259,3},{4... | collective-permute-start | bytes 2162696 | tf_op jit(solution)/shard_map/ppermute | solution.py:272

commit v5 on v4

--- a/solution.py
+++ b/solution.py
@@ -105,7 +105,7 @@
         real, imag = (sums[FRAMES + frame][:32] * kept, sums[FRAMES + frame][32:] * kept) if frame < CARRY else (empty, empty)
         rows[pl.ds(2 * FRAMES + frame, SLOTS, stride=MESSAGE), :] = real
         rows[pl.ds(2 * FRAMES + 4 + frame, SLOTS, stride=MESSAGE), :] = imag
-    out_ref[...] = rows[...].reshape(SLOTS, MESSAGE, LANES).astype(jnp.bfloat16)
+    out_ref[...] = rows[pl.ds(0, SLOTS * MESSAGE), :].reshape(SLOTS, MESSAGE, LANES).astype(jnp.bfloat16)
 
 
 def with_carry(real, imag, carried):
@@ -143,7 +143,8 @@
 
 def joined(ref, place):
     start = place * SLICE if isinstance(place, int) else pl.multiple_of(place * SLICE, SLICE)
-    wide = ref[:, pl.ds(start, SLICE), :].astype(jnp.float32)
+    block = ref[:, pl.ds(start, SLICE), :]
+    early = block[:, :16].astype(jnp.float32)
     sums = ref[: GROUPS - 1, pl.ds(HELD * SLICE, 32), :].astype(jnp.float32)
     sums = [sums[:, 8 * i : 8 * i + 8] for i in range(4)]
     if not isinstance(place, int):
@@ -154,12 +155,12 @@
         row = lax.broadcasted_iota(jnp.int32, sums[0].shape, 1) % 4
         carried = sum(jnp.where(row == i, pltpu.roll(sums[i], 5 + i, 1), 0.0) for i in range(CARRY))
     carried = jnp.concatenate([jnp.zeros((1, 8, LANES), jnp.float32), carried], 0)
-    real, imag = with_carry(wide[:, :8], wide[:, 8:16], carried)
-    return jnp.concatenate([real, imag, wide[:, 16:]], 1).reshape(GROUPS * SLICE, LANES)
+    early = jnp.concatenate(with_carry(early[:, :8], early[:, 8:], carried), 1).astype(jnp.bfloat16)
+    return jnp.concatenate([early, block[:, 16:]], 1).reshape(GROUPS * SLICE, LANES)
 
 
 def columns(ref, pair):
-    return jnp.concatenate([joined(ref, 2 * pair + i).astype(jnp.bfloat16) for i in range(2)], 1)
+    return jnp.concatenate([joined(ref, 2 * pair + i) for i in range(2)], 1)
 
 
 def own_kernel(own_ref, left_ref, prod_ref):
@@ -167,12 +168,12 @@
     same = same.astype(jnp.float32).astype(jnp.bfloat16)
     depth = GROUPS * 64
     for kind, place in enumerate((lax.axis_index("zh"), HELD - 1)):
-        wide = joined(own_ref, place)
-        split = wide.reshape(depth // 16, 16, LANES)
-        turned = jnp.concatenate([split[:, 8:], -split[:, :8]], 1).reshape(depth, LANES)
-        for half, value in enumerate((wide, turned)):
+        straight = joined(own_ref, place)
+        split = straight.astype(jnp.float32).reshape(depth // 16, 16, LANES)
+        turned = jnp.concatenate([split[:, 8:], -split[:, :8]], 1).reshape(depth, LANES).astype(jnp.bfloat16)
+        for half, value in enumerate((straight, turned)):
             left_ref[pl.ds(kind * 256 + half * LANES, LANES), :] = lax.dot_general(
-                same, value.astype(jnp.bfloat16), NT, preferred_element_type=jnp.float32
+                same, value, NT, preferred_element_type=jnp.float32
             ).astype(jnp.bfloat16)
     for pair in range(2):
         prod_ref[:, pl.ds(pair * 256, 256)] = jnp.dot(
@@ -253,7 +254,7 @@
             VMEM((FRAMES // 2, 2 * IN_DEV, FRAME_SAMPLES), bf16),
             VMEM((TAPS * 64, FRAME_SAMPLES), bf16),
             VMEM((IN_DEV, NCHAN), jnp.int32),
-            VMEM((SLOTS * MESSAGE, LANES), f32),
+            VMEM(((SLOTS + 1) * MESSAGE, LANES), f32),
             pltpu.SemaphoreType.DMA((FRAMES + 3,)),
         ],
         compiler_params=limit(16),

time: 74.9 us -> 74.9 us (level)
  no operation moved by 1% of the time
where the time goes in v5:
time: 74.9 us; the launch traced here: 74.7 us
  blocking collectives  60.9 us (81%)
  starting transfers between devices  6.59 us (9%)
  Pallas kernels  5.94 us (8%)
  waiting for transfers between devices  1.19 us (2%)
    all_to_all x1, blocking collectives, on_device(): lax.all_to_all(packed, ('zh', 'zl'), split_axis=0, concat_axis=0, tiled=T...  27.8 us
    all_to_all x1, blocking collectives, on_device(): lax.all_to_all(slotted, ('chan', 'x'), split_axis=0, concat_axis=0, tiled...  20.2 us
    all_to_all x1, blocking collectives, on_device(): lax.all_to_all(rows, ('zl', 'x'), split_axis=0, concat_axis=0, tiled=True)  12.9 us
    ppermute x1, starting transfers between devices, on_device(): other = lax.ppermute(own, 'inp', [(0, 1), (1, 0)])  6.59 us
    pallas_call x1, Pallas kernels, on_device(): pl.pallas_call(spectra_kernel, out_shape=VMEM((SLOTS, MESSAGE, LANES), bf...  3.39 us
  transfers between devices with their start and end apart: 1, of which 1 were waited for; matrix products, arithmetic and copies ran while one was open for 0% of the time, Pallas kernels for 1%

profile of v5, /device:TPU:1, one launch (start us, length us, event | category | flops | bytes accessed | tf_op | source)
XLA Modules:
  0.0 74.7 jit_solution(2853205888520910196)
XLA Ops:
  0.0 3.4 %spectra.1 = bf16[32,24,128]{2,1,0:T(8,128)(2,1)S(1)} custom-call(s32[1,1024]{1,0:T(1,128)} %bitcast.4, f32[4,2048]{1,0:T(4,128)} %constant.2.clone.window_hbm, s32[128,1024]{1,0:T(8,128)} %flags_hbm.1, bf16[128,16384]{1,0:T(8,128)(2,1)} %volts_hbm.1), custom_call_target="tpu_custom_call" | custom-call | tf_op jit(solution)/shard_map/spectra/pallas_call | solution.py:246
  3.4 20.2 %all_to_all.15.in_ref = bf16[32,24,128]{2,1,0:T(8,128)(2,1)S(1)} all-to-all(bf16[32,24,128]{2,1,0:T(8,128)(2,1)S(1)} %spectra.1), channel_id=1, replica_groups=mesh['inp'=2,'chan'=8,'zh'=4,'zl'=2,'x'=4] {'chan','x'}, dimensions={0} | all-to-all | bytes 393216 | tf_op jit(solution)/shard_map/all_to_all | solution.py:263
  23.6 0.1 pack.1
  23.7 27.8 %all_to_all.16.own_ref = bf16[8,352,128]{2,1,0:T(8,128)(2,1)S(1)} all-to-all(bf16[8,352,128]{2,1,0:T(8,128)(2,1)S(1)} %pack.1), channel_id=1, replica_groups=mesh['inp'=2,'chan'=8,'zh'=4,'zl'=2,'x'=4] {'zh','zl'}, dimensions={0} | all-to-all | bytes 1441792 | tf_op jit(solution)/shard_map/all_to_all | solution.py:272
  51.5 6.6 %collective-permute-start = (bf16[8,352,128]{2,1,0:T(8,128)(2,1)S(1)}, bf16[8,352,128]{2,1,0:T(8,128)(2,1)S(1)}, u32[]{:S(2)}, u32[]{:S(2)}) collective-permute-start(bf16[8,352,128]{2,1,0:T(8,128)(2,1)S(1)} %all_to_all.16.own_ref), channel_id=1, source_target_pairs={{0,256},{256,0},{1,257},{257,1},{2,258},{258,2},{3,259},{259,3},{4... | collective-permute-start | bytes 2162696 | tf_op jit(solution)/shard_map/ppermute | solution.py:273
  58.1 0.6 own.1
  58.7 1.2 %collective-permute-done.other_ref = bf16[8,352,128]{2,1,0:T(8,128)(2,1)S(1)} collective-permute-done((bf16[8,352,128]{2,1,0:T(8,128)(2,1)S(1)}, bf16[8,352,128]{2,1,0:T(8,128)(2,1)S(1)}, u32[]{:S(2)}, u32[]{:S(2)}) %collective-permute-start) | collective-permute-done | bytes 720928 | tf_op jit(solution)/shard_map/ppermute | solution.py:273
  59.9 0.7 other.1
  60.6 12.9 %all_to_all.17.in_ref = bf16[8,288,128]{2,1,0:T(8,128)(2,1)S(1)} all-to-all(bf16[8,288,128]{2,1,0:T(8,128)(2,1)S(1)} %other.1), channel_id=1, replica_groups=mesh['inp'=2,'chan'=8,'zh'=4,'zl'=2,'x'=4] {'zl','x'}, dimensions={0} | all-to-all | bytes 1179648 | tf_op jit(solution)/shard_map/all_to_all | solution.py:293
  73.5 1.1 %tiles.1 = f32[4,64,1088]{2,1,0:T(8,128)} custom-call(bf16[8,288,128]{2,1,0:T(8,128)(2,1)S(1)} %all_to_all.17.in_ref), custom_call_target="tpu_custom_call" | custom-call | tf_op jit(solution)/shard_map/tiles/pallas_call | solution.py:294
Async XLA Ops:
  51.5 8.4 %collective-permute-start = (bf16[8,352,128]{2,1,0:T(8,128)(2,1)S(1)}, bf16[8,352,128]{2,1,0:T(8,128)(2,1)S(1)}, u32[]{:S(2)}, u32[]{:S(2)}) collective-permute-start(bf16[8,352,128]{2,1,0:T(8,128)(2,1)S(1)} %all_to_all.16.own_ref), channel_id=1, source_target_pairs={{0,256},{256,0},{1,257},{257,1},{2,258},{258,2},{3,259},{259,3},{4... | collective-permute-start | bytes 2162696 | tf_op jit(solution)/shard_map/ppermute | solution.py:273

commit v6 on v5

--- a/solution.py
+++ b/solution.py
@@ -22,7 +22,9 @@
 HELD = 5
 MESSAGE = 24
 SLICE = 64
-BUNDLE = HELD * SLICE + 32
+SUMS = 4 * SLICE
+EXTRA = SUMS + 32
+BUNDLE = EXTRA + SLICE
 CUT = 18 * BLK
 PARCEL = 4 * 64 + 32
 CARRY = TAPS - 1
@@ -133,19 +135,22 @@
         extra = target + 1 - 2 * parity
         taken = [parity + 2 * i for i in range(4)]
         for place, group in enumerate(taken + [extra]):
-            out_ref[target, pl.ds(place * SLICE, SLICE), :] = slices[group]
+            out_ref[target, pl.ds(place * SLICE if place < 4 else EXTRA, SLICE), :] = slices[group]
         last = [
             jnp.where(unused, pltpu.roll(sums[extra], CARRY - i, 0), sums[group]) if i < CARRY else sums[group]
             for i, group in enumerate(taken)
         ]
-        out_ref[target, pl.ds(HELD * SLICE, 32), :] = jnp.concatenate(last, 0).astype(jnp.bfloat16)
+        out_ref[target, pl.ds(SUMS, 32), :] = jnp.concatenate(last, 0).astype(jnp.bfloat16)
 
 
 def joined(ref, place):
-    start = place * SLICE if isinstance(place, int) else pl.multiple_of(place * SLICE, SLICE)
+    if isinstance(place, int):
+        start = place * SLICE if place < 4 else EXTRA
+    else:
+        start = pl.multiple_of(place * SLICE, SLICE)
     block = ref[:, pl.ds(start, SLICE), :]
     early = block[:, :16].astype(jnp.float32)
-    sums = ref[: GROUPS - 1, pl.ds(HELD * SLICE, 32), :].astype(jnp.float32)
+    sums = ref[: GROUPS - 1, pl.ds(SUMS, 32), :].astype(jnp.float32)
     sums = [sums[:, 8 * i : 8 * i + 8] for i in range(4)]
     if not isinstance(place, int):
         carried = sum(jnp.where(place == i, sums[i], 0.0) for i in range(4))
@@ -270,7 +275,7 @@
         name="pack",
     )(placed)
     own = lax.all_to_all(packed, ("zh", "zl"), split_axis=0, concat_axis=0, tiled=True)
-    other = lax.ppermute(own, "inp", [(0, 1), (1, 0)])
+    other = lax.ppermute(own[:, :EXTRA], "inp", [(0, 1), (1, 0)])
     depth = GROUPS * 64
     left, prod = pl.pallas_call(
         own_kernel,

time: 74.9 us -> 74.8 us (level)
  no operation moved by 1% of the time
where the time goes in v6:
time: 74.8 us; the launch traced here: 74.6 us
  blocking collectives  60.9 us (81%)
  starting transfers between devices  6.61 us (9%)
  Pallas kernels  5.94 us (8%)
  waiting for transfers between devices  1 us (1%)
    all_to_all x1, blocking collectives, on_device(): lax.all_to_all(packed, ('zh', 'zl'), split_axis=0, concat_axis=0, tiled=T...  27.8 us
    all_to_all x1, blocking collectives, on_device(): lax.all_to_all(slotted, ('chan', 'x'), split_axis=0, concat_axis=0, tiled...  20.2 us
    all_to_all x1, blocking collectives, on_device(): lax.all_to_all(rows, ('zl', 'x'), split_axis=0, concat_axis=0, tiled=True)  12.9 us
    ppermute x1, starting transfers between devices, on_device(): other = lax.ppermute(own[:, :EXTRA], 'inp', [(0, 1), (1, 0)])  6.61 us
    pallas_call x1, Pallas kernels, on_device(): pl.pallas_call(spectra_kernel, out_shape=VMEM((SLOTS, MESSAGE, LANES), bf...  3.39 us
  transfers between devices with their start and end apart: 1, of which 1 were waited for; matrix products, arithmetic and copies ran while one was open for 0% of the time, Pallas kernels for 1%

profile of v6, /device:TPU:1, one launch (start us, length us, event | category | flops | bytes accessed | tf_op | source)
XLA Modules:
  0.0 74.6 jit_solution(16039314632337958159)
XLA Ops:
  0.0 3.4 %spectra.1 = bf16[32,24,128]{2,1,0:T(8,128)(2,1)S(1)} custom-call(s32[1,1024]{1,0:T(1,128)} %bitcast.4, f32[4,2048]{1,0:T(4,128)} %constant.2.clone.window_hbm, s32[128,1024]{1,0:T(8,128)} %flags_hbm.1, bf16[128,16384]{1,0:T(8,128)(2,1)} %volts_hbm.1), custom_call_target="tpu_custom_call" | custom-call | tf_op jit(solution)/shard_map/spectra/pallas_call | solution.py:251
  3.4 20.2 %all_to_all.15.in_ref = bf16[32,24,128]{2,1,0:T(8,128)(2,1)S(1)} all-to-all(bf16[32,24,128]{2,1,0:T(8,128)(2,1)S(1)} %spectra.1), channel_id=1, replica_groups=mesh['inp'=2,'chan'=8,'zh'=4,'zl'=2,'x'=4] {'chan','x'}, dimensions={0} | all-to-all | bytes 393216 | tf_op jit(solution)/shard_map/all_to_all | solution.py:268
  23.6 0.1 pack.1
  23.7 27.8 %all_to_all.16.own_ref = bf16[8,352,128]{2,1,0:T(8,128)(2,1)S(1)} all-to-all(bf16[8,352,128]{2,1,0:T(8,128)(2,1)S(1)} %pack.1), channel_id=1, replica_groups=mesh['inp'=2,'chan'=8,'zh'=4,'zl'=2,'x'=4] {'zh','zl'}, dimensions={0} | all-to-all | bytes 1441792 | tf_op jit(solution)/shard_map/all_to_all | solution.py:277
  51.5 6.6 %collective-permute-start = (bf16[8,288,128]{2,1,0:T(8,128)(2,1)S(1)}, bf16[8,288,128]{2,1,0:T(8,128)(2,1)S(1)}, u32[]{:S(2)}, u32[]{:S(2)}) collective-permute-start(bf16[8,288,128]{2,1,0:T(8,128)(2,1)S(1)} %slice.4), channel_id=1, source_target_pairs={{0,256},{256,0},{1,257},{257,1},{2,258},{258,2},{3,259},{259,3},{4... | collective-permute-start | bytes 1769480 | tf_op jit(solution)/shard_map/ppermute | solution.py:278
  58.2 0.6 own.1
  58.8 1.0 %collective-permute-done.other_ref = bf16[8,288,128]{2,1,0:T(8,128)(2,1)S(1)} collective-permute-done((bf16[8,288,128]{2,1,0:T(8,128)(2,1)S(1)}, bf16[8,288,128]{2,1,0:T(8,128)(2,1)S(1)}, u32[]{:S(2)}, u32[]{:S(2)}) %collective-permute-start) | collective-permute-done | bytes 589856 | tf_op jit(solution)/shard_map/ppermute | solution.py:278
  59.8 0.7 other.1
  60.5 12.9 %all_to_all.17.in_ref = bf16[8,288,128]{2,1,0:T(8,128)(2,1)S(1)} all-to-all(bf16[8,288,128]{2,1,0:T(8,128)(2,1)S(1)} %other.1), channel_id=1, replica_groups=mesh['inp'=2,'chan'=8,'zh'=4,'zl'=2,'x'=4] {'zl','x'}, dimensions={0} | all-to-all | bytes 1179648 | tf_op jit(solution)/shard_map/all_to_all | solution.py:298
  73.4 1.1 %tiles.1 = f32[4,64,1088]{2,1,0:T(8,128)} custom-call(bf16[8,288,128]{2,1,0:T(8,128)(2,1)S(1)} %all_to_all.17.in_ref), custom_call_target="tpu_custom_call" | custom-call | tf_op jit(solution)/shard_map/tiles/pallas_call | solution.py:299
  (1 shorter events, 0.0 us)
Async XLA Ops:
  51.5 8.2 %collective-permute-start = (bf16[8,288,128]{2,1,0:T(8,128)(2,1)S(1)}, bf16[8,288,128]{2,1,0:T(8,128)(2,1)S(1)}, u32[]{:S(2)}, u32[]{:S(2)}) collective-permute-start(bf16[8,288,128]{2,1,0:T(8,128)(2,1)S(1)} %slice.4), channel_id=1, source_target_pairs={{0,256},{256,0},{1,257},{257,1},{2,258},{258,2},{3,259},{259,3},{4... | collective-permute-start | bytes 1769480 | tf_op jit(solution)/shard_map/ppermute | solution.py:278

commit v7 on v6

--- a/solution.py
+++ b/solution.py
@@ -168,7 +168,18 @@
     return jnp.concatenate([joined(ref, 2 * pair + i) for i in range(2)], 1)
 
 
-def own_kernel(own_ref, left_ref, prod_ref):
+def put(ring, group, value):
+    for block in range(16):
+        skipped = (block + 3) % 4 * BLK
+        for i in range(2):
+            part = value[block * BLK : (block + 1) * BLK, i * LANES : (i + 1) * LANES]
+            part = (pltpu.roll(part, LANES - skipped, 1) if skipped else part).astype(jnp.bfloat16)
+            ring[pl.ds(block * BLK, BLK), pl.ds((group + 1 + i) * LANES, LANES)] = part
+            if group + i in (0, 7):
+                ring[pl.ds(block * BLK, BLK), pl.ds((9 if group + i == 0 else 0) * LANES, LANES)] = part
+
+
+def own_kernel(own_ref, left_ref, ring_ref):
     same = lax.broadcasted_iota(jnp.int32, (LANES, LANES), 0) == lax.broadcasted_iota(jnp.int32, (LANES, LANES), 1)
     same = same.astype(jnp.float32).astype(jnp.bfloat16)
     depth = GROUPS * 64
@@ -181,20 +192,16 @@
                 same, value, NT, preferred_element_type=jnp.float32
             ).astype(jnp.bfloat16)
     for pair in range(2):
-        prod_ref[:, pl.ds(pair * 256, 256)] = jnp.dot(
-            left_ref[...], columns(own_ref, pair), preferred_element_type=jnp.float32
-        )
-
-
-def other_kernel(left_ref, prod_ref, other_ref, out_ref, ring):
+        value = jnp.dot(left_ref[...], columns(own_ref, pair), preferred_element_type=jnp.float32)
+        put(ring_ref, 2 * pair, value)
+
+
+def other_kernel(left_ref, own_ring_ref, other_ref, out_ref, ring):
+    del own_ring_ref
     zh, zl = lax.axis_index("zh"), lax.axis_index("zl")
-    ring[:, pl.ds(LANES, 4 * LANES)] = prod_ref[...]
-    ring[:, pl.ds(9 * LANES, LANES)] = prod_ref[:, :LANES]
     for pair in range(2):
         value = jnp.dot(left_ref[...], columns(other_ref, pair), preferred_element_type=jnp.float32)
-        ring[:, pl.ds((5 + 2 * pair) * LANES, 2 * LANES)] = value
-        if pair == 1:
-            ring[:, pl.ds(0, LANES)] = value[:, LANES:]
+        put(ring, 4 + 2 * pair, value)
     lane = lax.broadcasted_iota(jnp.int32, (BLK, LANES), 1)
     for kind in range(2):
         target = (zl if kind == 0 else 1 - zl) * 4
@@ -205,15 +212,15 @@
             leads = (kind == 0) == (x > 0)
             lasts = []
             for half in range(2):
-                value = ring[pl.ds(kind * 256 + half * LANES + x * BLK, BLK), pl.ds(start, 5 * LANES)]
-                groups = [value[:, i * LANES : (i + 1) * LANES] for i in range(5)]
-                if skipped:
-                    groups = [pltpu.roll(group, LANES - skipped, 1) for group in groups]
-                lasts.append(groups[4][:, : LANES // 2])
+                row = kind * 256 + half * LANES + x * BLK
+                groups = [ring[pl.ds(row, BLK), pl.ds(start + i * LANES, LANES)] for i in range(5)]
+                fifth = groups[4].astype(jnp.float32)
+                lasts.append(fifth[:, : LANES // 2])
                 if leads and skipped:
-                    groups[0] = jnp.where(lane < LANES - skipped, groups[0], groups[4])
+                    head = jnp.where(lane < LANES - skipped, groups[0].astype(jnp.float32), fifth)
+                    groups[0] = head.astype(jnp.bfloat16)
                 for tile in range(4):
-                    out_ref[target + x, pl.ds(tile * 64 + half * BLK, BLK), :] = groups[tile].astype(jnp.bfloat16)
+                    out_ref[target + x, pl.ds(tile * 64 + half * BLK, BLK), :] = groups[tile]
             out_ref[target + x, pl.ds(256, BLK), :] = jnp.concatenate(lasts, 1).astype(jnp.bfloat16)
 
 
@@ -277,24 +284,27 @@
     own = lax.all_to_all(packed, ("zh", "zl"), split_axis=0, concat_axis=0, tiled=True)
     other = lax.ppermute(own[:, :EXTRA], "inp", [(0, 1), (1, 0)])
     depth = GROUPS * 64
-    left, prod = pl.pallas_call(
+    left, ring = pl.pallas_call(
         own_kernel,
-        out_shape=(jax.ShapeDtypeStruct((512, depth), bf16), jax.ShapeDtypeStruct((512, 4 * LANES), f32)),
+        out_shape=(jax.ShapeDtypeStruct((512, depth), bf16), jax.ShapeDtypeStruct((512, 10 * LANES), bf16)),
         in_specs=[vmem],
         out_specs=(vmem, vmem),
         compiler_params=limit(8),
         cost_estimate=pl.CostEstimate(flops=2 * 512 * 512 * 512, bytes_accessed=3 * 2**20, transcendentals=0),
         name="own",
     )(own)
-    rows = pl.pallas_call(
+    rows, _ = pl.pallas_call(
         other_kernel,
-        out_shape=jax.ShapeDtypeStruct((8, PARCEL, LANES), bf16),
+        out_shape=(
+            jax.ShapeDtypeStruct((8, PARCEL, LANES), bf16),
+            jax.ShapeDtypeStruct((512, 10 * LANES), bf16),
+        ),
         in_specs=[vmem, vmem, vmem],
-        out_specs=vmem,
-        scratch_shapes=[VMEM((512, 10 * LANES), f32)],
+        out_specs=(vmem, vmem),
+        input_output_aliases={1: 1},
         compiler_params=limit(12),
         name="other",
-    )(left, prod, other)
+    )(left, ring, other)
     parts = lax.all_to_all(rows, ("zl", "x"), split_axis=0, concat_axis=0, tiled=True)
     tiles = pl.pallas_call(
         tiles_kernel,

time: 74.8 us -> 74.8 us (level)
  no operation moved by 1% of the time
where the time goes in v7:
time: 74.8 us; the launch traced here: 74.6 us
  blocking collectives  61 us (82%)
  starting transfers between devices  6.61 us (9%)
  Pallas kernels  6 us (8%)
  waiting for transfers between devices  0.93 us (1%)
    all_to_all x1, blocking collectives, on_device(): lax.all_to_all(packed, ('zh', 'zl'), split_axis=0, concat_axis=0, tiled=T...  27.8 us
    all_to_all x1, blocking collectives, on_device(): lax.all_to_all(slotted, ('chan', 'x'), split_axis=0, concat_axis=0, tiled...  20.2 us
    all_to_all x1, blocking collectives, on_device(): lax.all_to_all(rows, ('zl', 'x'), split_axis=0, concat_axis=0, tiled=True)  12.9 us
    ppermute x1, starting transfers between devices, on_device(): other = lax.ppermute(own[:, :EXTRA], 'inp', [(0, 1), (1, 0)])  6.61 us
    pallas_call x1, Pallas kernels, on_device(): pl.pallas_call(spectra_kernel, out_shape=VMEM((SLOTS, MESSAGE, LANES), bf...  3.39 us
  transfers between devices with their start and end apart: 1, of which 1 were waited for; matrix products, arithmetic and copies ran while one was open for 0% of the time, Pallas kernels for 1%

profile of v7, /device:TPU:1, one launch (start us, length us, event | category | flops | bytes accessed | tf_op | source)
XLA Modules:
  0.0 74.6 jit_solution(5405685841410710232)
XLA Ops:
  0.0 3.4 %spectra.1 = bf16[32,24,128]{2,1,0:T(8,128)(2,1)S(1)} custom-call(s32[1,1024]{1,0:T(1,128)} %bitcast.4, f32[4,2048]{1,0:T(4,128)} %constant.2.clone.window_hbm, s32[128,1024]{1,0:T(8,128)} %flags_hbm.1, bf16[128,16384]{1,0:T(8,128)(2,1)} %volts_hbm.1), custom_call_target="tpu_custom_call" | custom-call | tf_op jit(solution)/shard_map/spectra/pallas_call | solution.py:258
  3.4 20.2 %all_to_all.15.in_ref = bf16[32,24,128]{2,1,0:T(8,128)(2,1)S(1)} all-to-all(bf16[32,24,128]{2,1,0:T(8,128)(2,1)S(1)} %spectra.1), channel_id=1, replica_groups=mesh['inp'=2,'chan'=8,'zh'=4,'zl'=2,'x'=4] {'chan','x'}, dimensions={0} | all-to-all | bytes 393216 | tf_op jit(solution)/shard_map/all_to_all | solution.py:275
  23.6 0.1 pack.1
  23.7 27.8 %all_to_all.16.own_ref = bf16[8,352,128]{2,1,0:T(8,128)(2,1)S(1)} all-to-all(bf16[8,352,128]{2,1,0:T(8,128)(2,1)S(1)} %pack.1), channel_id=1, replica_groups=mesh['inp'=2,'chan'=8,'zh'=4,'zl'=2,'x'=4] {'zh','zl'}, dimensions={0} | all-to-all | bytes 1441792 | tf_op jit(solution)/shard_map/all_to_all | solution.py:284
  51.5 6.6 %collective-permute-start = (bf16[8,288,128]{2,1,0:T(8,128)(2,1)S(1)}, bf16[8,288,128]{2,1,0:T(8,128)(2,1)S(1)}, u32[]{:S(2)}, u32[]{:S(2)}) collective-permute-start(bf16[8,288,128]{2,1,0:T(8,128)(2,1)S(1)} %slice.4), channel_id=1, source_target_pairs={{0,256},{256,0},{1,257},{257,1},{2,258},{258,2},{3,259},{259,3},{4... | collective-permute-start | bytes 1769480 | tf_op jit(solution)/shard_map/ppermute | solution.py:285
  58.2 0.7 own.1
  58.8 0.9 %collective-permute-done.other_ref = bf16[8,288,128]{2,1,0:T(8,128)(2,1)S(1)} collective-permute-done((bf16[8,288,128]{2,1,0:T(8,128)(2,1)S(1)}, bf16[8,288,128]{2,1,0:T(8,128)(2,1)S(1)}, u32[]{:S(2)}, u32[]{:S(2)}) %collective-permute-start) | collective-permute-done | bytes 589856 | tf_op jit(solution)/shard_map/ppermute | solution.py:285
  59.8 0.7 other.1
  60.5 12.9 %all_to_all.17.in_ref = bf16[8,288,128]{2,1,0:T(8,128)(2,1)S(1)} all-to-all(bf16[8,288,128]{2,1,0:T(8,128)(2,1)S(1)} %get-tuple-element.10), channel_id=1, replica_groups=mesh['inp'=2,'chan'=8,'zh'=4,'zl'=2,'x'=4] {'zl','x'}, dimensions={0} | all-to-all | bytes 1179648 | tf_op jit(solution)/shard_map/all_to_all | solution.py:308
  73.4 1.1 %tiles.1 = f32[4,64,1088]{2,1,0:T(8,128)} custom-call(bf16[8,288,128]{2,1,0:T(8,128)(2,1)S(1)} %all_to_all.17.in_ref), custom_call_target="tpu_custom_call" | custom-call | tf_op jit(solution)/shard_map/tiles/pallas_call | solution.py:309
  (1 shorter events, 0.0 us)
Async XLA Ops:
  51.5 8.2 %collective-permute-start = (bf16[8,288,128]{2,1,0:T(8,128)(2,1)S(1)}, bf16[8,288,128]{2,1,0:T(8,128)(2,1)S(1)}, u32[]{:S(2)}, u32[]{:S(2)}) collective-permute-start(bf16[8,288,128]{2,1,0:T(8,128)(2,1)S(1)} %slice.4), channel_id=1, source_target_pairs={{0,256},{256,0},{1,257},{257,1},{2,258},{258,2},{3,259},{259,3},{4... | collective-permute-start | bytes 1769480 | tf_op jit(solution)/shard_map/ppermute | solution.py:285
